TPU v7x, 32 devices: a whole 2x2x4 slice. The times are simulated.
32 devices in a mesh: ctx: 8 (over z, x), head: 4 (over y, core).
Axes of the slice: x: 2, y: 2, z: 4, core: 2. Of those that a mesh axis runs over, the one named last changes fastest.
Arguments:
- queries: bfloat16 [8192, 5120], P('ctx', 'head'), may hold values from -60 to 60
- key_rows: bfloat16 [8192, 5120], P('ctx', 'head'), may hold values from -10 to 10
- value_rows: bfloat16 [8192, 5120], P('ctx', 'head'), may hold values from -60 to 60
- norm_gain: float32 [5120], P('head'), may hold values from 0.1 to 1.9
- sort_index: int32 [32], replicated, may hold values from 0 to 31
- grad_normed: bfloat16 [8192, 5120], P('ctx', 'head'), may hold values from -6 to 6
Outputs:
- normed: bfloat16 [8192, 5120], P('ctx', 'head')
- grad_queries: bfloat16 [8192, 5120], P('ctx', 'head')
- grad_keys: bfloat16 [8192, 5120], P('ctx', 'head')
- grad_values: bfloat16 [8192, 5120], P('ctx', 'head')
Inputs may be any that keep to these rules, and one draw needn't show every extreme that they name: `sort_index`: several query blocks may name the same block.
All inputs are finite; a program needn't handle non-finite values.
Results may differ from a plain program's by a relative error of at most 0.009.
Values may be sent and summed in bfloat16 or wider, within the bound.
No kernel may reach another device: no remote copies, remote signals or barrier semaphores. Data moves between devices by JAX's collectives and lax.ppermute only.
A program may use at most 128 MiB of HBM per device.

v0:
```python
import functools
import math

import jax
import jax.numpy as jnp
import numpy as np
from jax import lax
from jax.experimental import pallas as pl
from jax.experimental.pallas import tpu as pltpu
from jax.sharding import PartitionSpec as P

HDIM = 128
BLOCK = 256
WIDTH = 5120
LANES = 128
ROW = 16
LEAD = 2
FIRST = 1024
STATIC_SLOTS = 9
SCALE = HDIM ** (-0.5)
SCALE_LOG2 = SCALE * math.log2(math.e)
ANY = pl.BlockSpec(memory_space=pl.ANY)
SMEM = pl.BlockSpec(memory_space=pltpu.SMEM)
VMEM = pl.BlockSpec(memory_space=pltpu.VMEM)
BIG = pltpu.CompilerParams(vmem_limit_bytes=56 * 1024 * 1024)
MOVE = pltpu.CompilerParams(vmem_limit_bytes=56 * 1024 * 1024)


class Layout:
    def __init__(self, ctx_size, blocks):
        self.ctx_size = ctx_size
        self.blocks = blocks
        self.levels = ctx_size // 2
        line = self.levels * blocks
        self.value_line = line
        self.value_own = 2 * line
        self.over = 2 * line + blocks
        self.places = self.over + 2 * (blocks + 1)
        self.slots = 2 * (2 * line + 2 * self.levels + 2 * blocks + 4)
        self.rows = self.slots + 2 * LEAD
        self.info = self.rows * ROW
        self.key_picks = self.info
        self.value_picks = self.info + blocks + 1
        self.total = self.info + 2 * blocks + 2
        self.device = self.info + 2 * blocks + 3


def shift_rows(array, count, rows):
    n = array.shape[0]
    if abs(count) >= n:
        return jnp.zeros_like(array)
    rolled = pltpu.roll(array, (-count) % n, 0)
    inside = (rows < n - count) if count > 0 else (rows >= -count)
    return jnp.where(inside, rolled, 0.0)


def table_kernel(picks_ref, gain_ref, out_ref, gain_row_ref, *, lay):
    n = lay.ctx_size
    blocks = lay.blocks
    count = n * blocks
    width = -(-2 * count // LANES) * LANES
    rows = lax.broadcasted_iota(jnp.int32, (n, width), 0)
    lanes = lax.broadcasted_iota(jnp.int32, (n, width), 1)
    out_lanes = lax.broadcasted_iota(jnp.int32, (n, LANES), 1)
    values = lanes >= count
    block = jnp.where(lanes >= 2 * count, -2, jnp.where(values, lanes - count, lanes))
    owner = jnp.floor((block.astype(jnp.float32) + 0.5) / blocks).astype(jnp.int32)
    within = block - owner * blocks
    line = (owner >> 1) * blocks + within
    place = jnp.where(values, jnp.where(owner == rows, lay.value_own + within, lay.value_line + line), line)
    place = jnp.where(block < 0, 0, place).astype(jnp.float32)
    picks = picks_ref[...]
    side = rows & 1
    level = rows >> 1
    same_side = side == (owner & 1)
    travels = jnp.logical_xor(same_side, values)
    owned = owner == rows

    def other(array):
        return jnp.where(side == 0, pltpu.roll(array, n - 1, 0), pltpu.roll(array, 1, 0))

    need = jnp.zeros((n, width), jnp.float32)
    for j in range(blocks + 1):
        need = jnp.where(picks[:, j : j + 1] == block, 1.0, need)
    need = jnp.where(owned, 0.0, need)
    across = other(need)
    wanted = jnp.maximum(need, across)
    final = jnp.where(travels, across, 0.0)
    hops = jnp.where(wanted > 0, 1.0 + final, 0.0)
    up_hops = jnp.zeros_like(need)
    down_hops = jnp.zeros_like(need)
    for k in range(1, lay.levels):
        above = shift_rows(hops, 2 * k, rows)
        below = shift_rows(hops, -2 * k, rows)
        up_hops = jnp.maximum(up_hops, jnp.where(above > 0, above + (k - 1), 0.0))
        down_hops = jnp.maximum(down_hops, jnp.where(below > 0, below + (k - 1), 0.0))
    up = jnp.where(travels & (level >= (owner >> 1)) & (up_hops > 0), 1.0, 0.0)
    down = jnp.where(travels & (level <= (owner >> 1)) & (down_hops > 0), 1.0, 0.0)
    source = owned & jnp.logical_not(travels)
    most = jnp.maximum(up_hops, down_hops)
    over = jnp.where(source & ((most > 0) | (across > 0)), 1.0, final)
    spread = jnp.minimum(jnp.sum(need, axis=0, keepdims=True), 3.0)
    low = (width - 1 - lanes).astype(jnp.float32)
    up_rank = (up_hops * 4.0 + spread) * width + low
    down_rank = (down_hops * 4.0 + spread) * width + low
    over_rank = jnp.where(source, most * 4.0 + spread, 2.0) * width + low
    first_over = float(lay.over)

    gain_row_ref[0, :] = gain_ref[:]
    out_ref[...] = jnp.full(out_ref.shape, -1, jnp.int32)

    def pick(pending, have, rank):
        score = jnp.where(pending * have > 0, rank, -1.0)
        best = jnp.max(score, axis=1, keepdims=True)
        return jnp.where((score == best) & (best >= 0), 1.0, 0.0)

    def where(chosen):
        return jnp.sum(chosen * (place + 1.0), axis=1, keepdims=True) - 1.0

    def pending(state):
        t, have, fresh, up, down, over, over_place, count = state
        return (t < lay.slots) & (jnp.sum(up + down + over) > 0)

    def step(state):
        t, have, fresh, up, down, over, over_place, count = state
        send_up = pick(up, have, up_rank)
        send_down = pick(down, have, down_rank)
        send_over = pick(over, have, over_rank)
        up = up - send_up
        down = down - send_down
        over = over - send_over
        got_up = shift_rows(send_up, -2, rows)
        got_down = shift_rows(send_down, 2, rows)
        got_over = other(send_over)
        got_final = jnp.where(travels, 0.0, got_over)
        any_final = jnp.max(got_final, axis=1, keepdims=True)
        over_at = jnp.where(any_final > 0, count + first_over, where(got_over))
        last = jnp.where((up + down + over + need > 0) | owned, 0.0, float(FIRST))

        def first_back(chosen):
            return jnp.max(chosen * last, axis=1, keepdims=True)

        columns = (
            where(send_up) + first_back(send_up),
            where(send_down) + first_back(send_down * (1.0 - send_up)),
            where(send_over) + first_back(send_over * (1.0 - send_up) * (1.0 - send_down)),
            where(got_up),
            where(got_down),
            over_at,
        )
        row = jnp.full((n, LANES), -1.0, jnp.float32)
        for k, column in enumerate(columns):
            row = jnp.where(out_lanes == k, column, row)
        out_ref[t + LEAD] = row.astype(jnp.int32)
        over_place = jnp.where(got_final > 0, count + first_over, over_place)
        have = jnp.maximum(have, fresh)
        fresh = jnp.maximum(got_up, jnp.maximum(got_down, got_over))
        return (t + 1, have, fresh, up, down, over, over_place, count + any_final)

    zeros = jnp.zeros_like(need)
    have = jnp.where(owned, 1.0, 0.0)
    state = (jnp.int32(0), have, zeros, up, down, over, zeros, jnp.zeros((n, 1), jnp.float32))
    state = lax.while_loop(pending, step, state)
    at = jnp.where(travels | owned, place, state[6])
    own_row = lax.broadcasted_iota(jnp.int32, (n, LANES), 0)
    row = jnp.zeros((n, LANES), jnp.float32)
    for kind in range(2):
        base = (own_row >> 1) * blocks if kind == 0 else jnp.full((n, LANES), lay.value_own)
        for j in range(blocks + 1):
            chosen = (picks[:, j : j + 1] == block) & (values if kind else jnp.logical_not(values))
            found = jnp.sum(jnp.where(chosen, at, 0.0), axis=1, keepdims=True)
            found = jnp.where(picks[:, j : j + 1] < 0, base[:, :1].astype(jnp.float32), found)
            row = jnp.where(out_lanes == kind * (blocks + 1) + j, found, row)
    row = jnp.where(out_lanes == 2 * blocks + 2, state[0].astype(jnp.float32), row)
    row = jnp.where(out_lanes == 2 * blocks + 3, own_row.astype(jnp.float32), row)
    out_ref[lay.rows] = row.astype(jnp.int32)


def routing_table(sort_index, norm_gain, lay):
    n, blocks = lay.ctx_size, lay.blocks
    before = (np.arange(n, dtype=np.int32) * blocks - 1)[:, None]
    picks = jnp.concatenate([sort_index.reshape(n, blocks), jnp.asarray(before)], axis=1)
    picks = jnp.pad(picks, ((0, 0), (0, LANES - blocks - 1)), constant_values=-1)
    table, gain = pl.pallas_call(
        functools.partial(table_kernel, lay=lay),
        out_shape=(
            jax.ShapeDtypeStruct((lay.rows + 1, n, LANES), jnp.int32),
            jax.ShapeDtypeStruct((1,) + norm_gain.shape, norm_gain.dtype),
        ),
        in_specs=[VMEM, VMEM],
        out_specs=(VMEM, VMEM),
        name="routing_table",
    )(picks, norm_gain)
    mine = lax.dynamic_slice(table, (0, lax.axis_index("ctx"), 0), (lay.rows + 1, 1, ROW))
    return mine.reshape((lay.rows + 1) * ROW), gain


def routes(ctx_size):
    up = [(d, d + 2) for d in range(ctx_size - 2)]
    down = [(d + 2, d) for d in range(ctx_size - 2)]
    over = [(d, d ^ 1) for d in range(ctx_size)]
    return up, down, over


def copies(jobs, sems):
    started = []
    for k, (valid, source, target) in enumerate(jobs):
        copy = pltpu.make_async_copy(source, target, sems.at[k])
        pl.when(valid)(copy.start)
        started.append((valid, copy))
    for valid, copy in started:
        pl.when(valid)(copy.wait)


def entry(tab_ref, t, k):
    return tab_ref[(t + LEAD) * ROW + k]


def place_of(code):
    return jnp.maximum(code, 0) & (FIRST - 1)


def fill_kernel(tab_ref, key_ref, value_ref, pool_ref, held_ref, sems, *, lay):
    blocks = lay.blocks
    level = tab_ref[lay.device] >> 1
    loads = [
        pltpu.make_async_copy(key_ref, held_ref.at[pl.ds(0, blocks)], sems.at[0]),
        pltpu.make_async_copy(value_ref, held_ref.at[pl.ds(blocks, blocks)], sems.at[1]),
    ]
    stores = [
        pltpu.make_async_copy(
            held_ref.at[pl.ds(0, blocks)], pool_ref.at[pl.ds(level * blocks, blocks)], sems.at[2]
        ),
        pltpu.make_async_copy(
            held_ref.at[pl.ds(blocks, blocks)],
            pool_ref.at[pl.ds(lay.value_own, blocks)],
            sems.at[3],
        ),
    ]
    for load in loads:
        load.start()
    for load, store in zip(loads, stores):
        load.wait()
        store.start()
    for store in stores:
        store.wait()


def first_kernel(
    tab_ref, key_ref, value_ref, up_ref, down_ref, over_ref, held_ref, sems, *, lay, slot
):
    blocks = lay.blocks
    level = tab_ref[lay.device] >> 1
    loads, stores = [], []
    for k, out in enumerate((up_ref, down_ref, over_ref)):
        code = entry(tab_ref, slot, k)
        at = place_of(code)
        is_value = at >= lay.value_own
        key_at = jnp.clip(at - level * blocks, 0, blocks - 1)
        value_at = jnp.clip(at - lay.value_own, 0, blocks - 1)
        valid = code >= 0
        loads.append((valid & jnp.logical_not(is_value), key_ref.at[key_at], held_ref.at[k]))
        loads.append((valid & is_value, value_ref.at[value_at], held_ref.at[k]))
        stores.append((valid, held_ref.at[k], out))
    copies(loads, sems)
    copies(stores, sems)


def slot_and_rest(slot, refs):
    return (refs[0][0], refs[1:]) if slot is None else (slot, refs)


def match(place, valid, places, valids):
    hits = [valid & v & (place == p) for p, v in zip(places, valids)]
    found = hits[0] | hits[1] | hits[2]
    return found, jnp.where(hits[0], 0, jnp.where(hits[1], 1, 2))


def step_kernel(*refs, slot):
    t, refs = slot_and_rest(slot, refs)
    (
        tab_ref, _, in_up, in_down, in_over, pool_ref, up_ref, down_ref, over_ref, held_ref, sems,
    ) = refs
    got_codes = [entry(tab_ref, t - 2, 3 + k) for k in range(3)]
    got_valid = [c >= 0 for c in got_codes]
    got_places = [place_of(c) for c in got_codes]
    loads = [
        (v, got, held_ref.at[k])
        for k, (v, got) in enumerate(zip(got_valid, (in_up, in_down, in_over)))
    ]
    stores = [
        (v, held_ref.at[k], pool_ref.at[p])
        for k, (v, p) in enumerate(zip(got_valid, got_places))
    ]
    for k, out in enumerate((up_ref, down_ref, over_ref)):
        code = entry(tab_ref, t, k)
        valid = code >= 0
        place = place_of(code)
        found, at = match(place, valid, got_places, got_valid)
        loads.append((valid & jnp.logical_not(found), pool_ref.at[place], held_ref.at[3 + k]))
        stores.append((valid, held_ref.at[jnp.where(found, at, 3 + k)], out))
    copies(loads, sems)
    copies(stores, sems)


def close_kernel(*refs, slot, back):
    t, refs = slot_and_rest(slot, refs)
    tab_ref, _, in_up, in_down, in_over, pool_ref, held_ref, sems = refs
    loads, stores = [], []
    for k, got in enumerate((in_up, in_down, in_over)):
        code = entry(tab_ref, t - back, 3 + k)
        loads.append((code >= 0, got, held_ref.at[k]))
        stores.append((code >= 0, held_ref.at[k], pool_ref.at[place_of(code)]))
    copies(loads, sems)
    copies(stores, sems)


def traffic(byte_count):
    return pl.CostEstimate(flops=0, bytes_accessed=byte_count, transcendentals=0)


def send_all(sends, perms):
    return tuple(lax.ppermute(s, "ctx", p) for s, p in zip(sends, perms))


def numbered(kernel, t, call):
    known = isinstance(t, int)
    extra = [] if known else [t.reshape(1)]
    specs = [] if known else [SMEM]
    return functools.partial(
        pl.pallas_call(
            functools.partial(kernel, slot=t if known else None),
            in_specs=specs + call.pop("in_specs"),
            input_output_aliases={1 + len(extra): 0},
            compiler_params=MOVE,
            **call,
        ),
        *extra,
    )


def gather_blocks(keys, values, tab, lay):
    one = jax.ShapeDtypeStruct(keys.shape[1:], keys.dtype)
    pool_shape = jax.ShapeDtypeStruct((lay.places,) + one.shape, one.dtype)
    size = 2 * math.prod(one.shape)
    perms = routes(lay.ctx_size)
    six = [pltpu.VMEM((6,) + one.shape, one.dtype), pltpu.SemaphoreType.DMA((6,))]

    def first(slot):
        sends = pl.pallas_call(
            functools.partial(first_kernel, lay=lay, slot=slot),
            out_shape=(one,) * 3,
            in_specs=[SMEM, ANY, ANY],
            out_specs=(ANY,) * 3,
            scratch_shapes=six,
            compiler_params=MOVE,
            cost_estimate=traffic(size * 6),
            name="gather_first",
        )(tab, keys, values)
        return send_all(sends, perms)

    older = first(0)
    newer = first(1)
    pool = pl.pallas_call(
        functools.partial(fill_kernel, lay=lay),
        out_shape=pool_shape,
        in_specs=[SMEM, ANY, ANY],
        out_specs=ANY,
        scratch_shapes=[
            pltpu.VMEM((2 * lay.blocks,) + one.shape, one.dtype),
            pltpu.SemaphoreType.DMA((4,)),
        ],
        compiler_params=MOVE,
        cost_estimate=traffic(size * 4 * lay.blocks),
        name="gather_fill",
    )(tab, keys, values)

    def step(t, pool, got):
        call = dict(
            out_shape=(pool_shape, one, one, one),
            in_specs=[SMEM] + [ANY] * 4,
            out_specs=(ANY,) * 4,
            scratch_shapes=six,
            cost_estimate=traffic(size * 12),
            name="gather_step",
        )
        pool, *sends = numbered(step_kernel, t, call)(tab, pool, *got)
        return pool, send_all(sends, perms)

    for t in range(2, STATIC_SLOTS):
        pool, latest = step(t, pool, older)
        older, newer = newer, latest

    def body(state):
        t, pool, older, newer = state
        pool, latest = step(t, pool, older)
        return t + 1, pool, newer, latest

    t, pool, older, newer = lax.while_loop(
        lambda state: state[0] < tab[lay.total],
        body,
        (jnp.int32(STATIC_SLOTS), pool, older, newer),
    )
    for back, got in ((2, older), (1, newer)):
        call = dict(
            out_shape=pool_shape,
            in_specs=[SMEM] + [ANY] * 4,
            out_specs=ANY,
            scratch_shapes=six,
            cost_estimate=traffic(size * 6),
            name="gather_close",
        )
        pool = numbered(functools.partial(close_kernel, back=back), t, call)(tab, pool, *got)
    return pool


def add(target_ref, to, source_ref, at):
    target_ref[to] = (
        target_ref[to].astype(jnp.float32) + source_ref[at].astype(jnp.float32)
    ).astype(target_ref.dtype)


def back_kernel(*refs, slot):
    t, refs = slot_and_rest(slot, refs)
    (
        tab_ref, _, in_up, in_down, in_over, pool_ref, up_ref, down_ref, over_ref,
        held_ref, got_ref, sems,
    ) = refs
    codes = [entry(tab_ref, t + 2, k) for k in range(3)]
    places = [place_of(c) for c in codes]
    valid = [c >= 0 for c in codes]
    fresh = [c >= FIRST for c in codes]
    same_10 = valid[1] & valid[0] & (places[1] == places[0])
    same_20 = valid[2] & valid[0] & (places[2] == places[0])
    same_21 = valid[2] & valid[1] & (places[2] == places[1]) & jnp.logical_not(same_20)
    alone = [
        valid[0],
        valid[1] & jnp.logical_not(same_10),
        valid[2] & jnp.logical_not(same_20 | same_21),
    ]
    loads = [
        (v, got, got_ref.at[k]) for k, (v, got) in enumerate(zip(valid, (in_up, in_down, in_over)))
    ]
    loads += [
        (a & jnp.logical_not(f), pool_ref.at[p], held_ref.at[k])
        for k, (a, f, p) in enumerate(zip(alone, fresh, places))
    ]
    stores = []
    leaves = [False] * 3
    for k, out in enumerate((up_ref, down_ref, over_ref)):
        code = entry(tab_ref, t, 3 + k)
        takes = code >= 0
        place = place_of(code)
        found, at = match(place, takes, places, alone)
        loads.append((takes & jnp.logical_not(found), pool_ref.at[place], held_ref.at[3 + k]))
        stores.append((takes, held_ref.at[jnp.where(found, at, 3 + k)], out))
        leaves = [leave | (found & (at == n)) for n, leave in enumerate(leaves)]
    copies(loads, sems)
    for k in range(3):

        @pl.when(alone[k] & fresh[k])
        def _(k=k):
            held_ref[k] = got_ref[k]

        @pl.when(alone[k] & jnp.logical_not(fresh[k]))
        def _(k=k):
            add(held_ref, k, got_ref, k)

    for k, to, here in ((1, 0, same_10), (2, 0, same_20), (2, 1, same_21)):

        @pl.when(here)
        def _(k=k, to=to):
            add(held_ref, to, got_ref, k)

    stores += [
        (a & jnp.logical_not(leave), held_ref.at[k], pool_ref.at[p])
        for k, (a, leave, p) in enumerate(zip(alone, leaves, places))
    ]
    copies(stores, sems)


def home_kernel(tab_ref, pool_ref, *refs, lay):
    arrived, (key_ref, value_ref, own_ref, got_ref, sems) = refs[:6], refs[6:]
    blocks = lay.blocks
    level = tab_ref[lay.device] >> 1
    halves = (
        (pool_ref.at[pl.ds(level * blocks, blocks)], key_ref),
        (pool_ref.at[pl.ds(lay.value_own, blocks)], value_ref),
    )
    loads, stores = [], []
    for k, (source, target) in enumerate(halves):
        held = own_ref.at[pl.ds(k * blocks, blocks)]
        loads.append((level >= 0, source, held))
        stores.append((level >= 0, held, target))
    codes = [entry(tab_ref, 1 - n // 3, n % 3) for n in range(6)]
    for n, (code, got) in enumerate(zip(codes, arrived)):
        loads.append((code >= 0, got, got_ref.at[n]))
    copies(loads, sems)
    for n, code in enumerate(codes):
        place = place_of(code)
        at = jnp.where(
            place >= lay.value_own, place - lay.value_own + blocks, place - level * blocks
        )

        @pl.when(code >= 0)
        def _(n=n, at=at):
            add(own_ref, jnp.clip(at, 0, 2 * blocks - 1), got_ref, n)

    copies(stores, sems)


def return_blocks(pool, tab, lay):
    one = jax.ShapeDtypeStruct(pool.shape[1:], pool.dtype)
    pool_shape = jax.ShapeDtypeStruct(pool.shape, pool.dtype)
    own_shape = jax.ShapeDtypeStruct((lay.blocks,) + one.shape, one.dtype)
    size = 2 * math.prod(one.shape)
    up, down, over = routes(lay.ctx_size)
    perms = ([(b, a) for a, b in up], [(b, a) for a, b in down], over)

    def step(t, pool, got):
        call = dict(
            out_shape=(pool_shape, one, one, one),
            in_specs=[SMEM] + [ANY] * 4,
            out_specs=(ANY,) * 4,
            scratch_shapes=[
                pltpu.VMEM((6,) + one.shape, one.dtype),
                pltpu.VMEM((3,) + one.shape, one.dtype),
                pltpu.SemaphoreType.DMA((9,)),
            ],
            cost_estimate=traffic(size * 15),
            name="return_step",
        )
        pool, *sends = numbered(back_kernel, t, call)(tab, pool, *got)
        return pool, send_all(sends, perms)

    def body(state):
        t, pool, older, newer = state
        pool, latest = step(t, pool, older)
        return t - 1, pool, newer, latest

    nothing = (jnp.zeros(one.shape, one.dtype),) * 3
    _, pool, older, newer = lax.while_loop(
        lambda state: state[0] >= STATIC_SLOTS,
        body,
        (tab[lay.total] - 1, pool, nothing, nothing),
    )
    for t in range(STATIC_SLOTS - 1, -1, -1):
        pool, latest = step(t, pool, older)
        older, newer = newer, latest
    return pl.pallas_call(
        functools.partial(home_kernel, lay=lay),
        out_shape=(own_shape, own_shape),
        in_specs=[SMEM] + [ANY] * 7,
        out_specs=(ANY, ANY),
        scratch_shapes=[
            pltpu.VMEM((2 * lay.blocks,) + one.shape, one.dtype),
            pltpu.VMEM((6,) + one.shape, one.dtype),
            pltpu.SemaphoreType.DMA((8,)),
        ],
        compiler_params=MOVE,
        cost_estimate=traffic(size * 30),
        name="return_home",
    )(tab, pool, *older, *newer)


QK = (((1,), (1,)), ((), ()))
AB = (((1,), (0,)), ((), ()))
TA = (((0,), (0,)), ((), ()))


def dot(a, b, dims):
    return lax.dot_general(a, b, dims, preferred_element_type=jnp.float32)


def rows_of(i):
    return slice(i * BLOCK, (i + 1) * BLOCK)


def parts_of(i, cols, own_ref, pick_refs):
    blocks = len(pick_refs) - 1
    before = pick_refs[blocks][0, :, cols] if i == 0 else own_ref[i - 1, :, cols]
    return own_ref[i, :, cols], before, pick_refs[i][0, :, cols]


def term_places(tab_ref, lay):
    level = tab_ref[lay.device] >> 1
    result = []
    for base, picks in ((level * lay.blocks, lay.key_picks), (lay.value_own, lay.value_picks)):
        places = [base + o for o in range(lay.blocks)]
        places += [tab_ref[picks + j] for j in range(lay.blocks + 1)]
        result.append(places)
    return result


def forward_kernel(tab_ref, *refs, lay, group):
    blocks = lay.blocks
    count = blocks + 2
    q_ref, key_refs, value_refs = refs[0], refs[1 : 1 + count], refs[1 + count : 1 + 2 * count]
    gain_ref, grad_ref, attended_ref, probs_ref, sums_ref, acc_ref = refs[1 + 2 * count :]
    h = pl.program_id(0)
    causal = lax.broadcasted_iota(jnp.int32, (BLOCK, BLOCK), 0) <= lax.broadcasted_iota(
        jnp.int32, (BLOCK, BLOCK), 1
    )
    hide = jnp.where(tab_ref[lay.device] > 0, 0.0, -jnp.inf).astype(jnp.float32)
    lane = lax.broadcasted_iota(jnp.int32, (BLOCK, LANES), 1)

    @pl.when(h == 0)
    def _():
        acc_ref[...] = jnp.zeros_like(acc_ref)

    def score(i, g):
        cols = slice(g * HDIM, (g + 1) * HDIM)
        q = q_ref[rows_of(i), cols]
        return [dot(k, q, QK) for k in parts_of(i, cols, key_refs[0], key_refs[1:])]

    tasks = [(i, g) for i in range(blocks) for g in range(group)]
    following = score(*tasks[0])
    for n, (i, g) in enumerate(tasks):
        scores = following
        if n + 1 < len(tasks):
            following = score(*tasks[n + 1])
        cols = slice(g * HDIM, (g + 1) * HDIM)
        scores[0] = jnp.where(causal, scores[0], -jnp.inf)
        if i == 0:
            scores[1] = scores[1] + hide
        top = jnp.max(
            jnp.maximum(jnp.maximum(scores[0], scores[1]), scores[2]), axis=0, keepdims=True
        )
        weights = [jnp.exp2((s - top) * SCALE_LOG2) for s in scores]
        scale = 1.0 / jnp.sum(weights[0] + weights[1] + weights[2], axis=0, keepdims=True)
        turned = 0.0
        values = parts_of(i, cols, value_refs[0], value_refs[1:])
        for j, (w, v) in enumerate(zip(weights, values)):
            low = (w * scale).astype(jnp.bfloat16)
            probs_ref[i, g, rows_of(j)] = low
            turned += dot(v, low, TA)
        attended = jnp.transpose(turned)
        attended_ref[rows_of(i), cols] = attended
        lifted = gain_ref[:, cols] * grad_ref[rows_of(i), cols].astype(jnp.float32)
        squares = jnp.sum(attended * attended, axis=1, keepdims=True)
        center = jnp.sum(lifted * attended, axis=1, keepdims=True)
        acc_ref[i] += jnp.where(lane == 0, squares, jnp.where(lane == 1, center, 0.0))

    @pl.when(h == pl.num_programs(0) - 1)
    def _():
        for i in range(blocks):
            sums_ref[:, rows_of(i)] = jnp.transpose(acc_ref[i])[:8]


def backward_kernel(
    tab_ref, q_ref, pool_in, gain_ref, grad_ref, attended_ref, probs_ref, *refs, lay, group
):
    del pool_in
    sums_refs, refs = refs[:-9], refs[-9:]
    normed_ref, gq_ref, pool_ref, rms_ref, acc_ref, out_ref, kv_ref, sems, load_sems = refs
    blocks = lay.blocks
    h = pl.program_id(0)
    steps = pl.num_programs(0)
    width = group * HDIM
    terms = 2 * blocks + 1
    places = term_places(tab_ref, lay)
    buffer = lax.rem(h, 2)

    def columns(at):
        return pl.ds(pl.multiple_of(at * width, width), width)

    def loads(at, buffer):
        return [
            pltpu.make_async_copy(
                pool_ref.at[places[kind][n], :, columns(at)],
                kv_ref.at[buffer, kind, n],
                load_sems.at[buffer, kind * terms + n],
            )
            for kind in range(2)
            for n in range(terms)
        ]

    @pl.when(h == 0)
    def _():
        for load in loads(0, 0):
            load.start()

    for load in loads(h, buffer):
        load.wait()

    @pl.when(h + 1 < steps)
    def _():
        for load in loads(h + 1, 1 - buffer):
            load.start()

    @pl.when(h == 0)
    def _():
        sums = sum(ref[...] for ref in sums_refs)
        squares = sums[0:1]
        center = sums[1:2]
        inv = lax.rsqrt(squares / WIDTH + 1e-05)
        factor = inv * inv * inv * center / WIDTH
        both = jnp.concatenate([inv, factor, jnp.zeros((6,) + inv.shape[1:], jnp.float32)], axis=0)
        for i in range(blocks):
            wide = jnp.concatenate([both[:, rows_of(i)]] * (LANES // 8), axis=0)
            rms_ref[i] = jnp.transpose(wide)

    def places_in(i):
        return (i, 2 * blocks if i == 0 else i - 1, blocks + i)

    def prepare(i, g):
        cols = slice(g * HDIM, (g + 1) * HDIM)
        inv_rms = rms_ref[i, :, 0:1]
        factor = rms_ref[i, :, 1:2]
        attended = attended_ref[rows_of(i), cols]
        gain = gain_ref[:, cols]
        normed_ref[rows_of(i), cols] = (attended * inv_rms * gain).astype(jnp.bfloat16)
        lifted = gain * grad_ref[rows_of(i), cols].astype(jnp.float32)
        grad = (inv_rms * lifted - attended * factor).astype(jnp.bfloat16)
        row = jnp.sum(jnp.transpose(grad.astype(jnp.float32) * attended), axis=0, keepdims=True)
        gps = [dot(kv_ref[buffer, 1, n, :, cols], grad, QK) for n in places_in(i)]
        return grad, row, gps

    tasks = [(i, g) for i in range(blocks) for g in range(group)]
    following = prepare(*tasks[0])
    for n, (i, g) in enumerate(tasks):
        grad, row, gps = following
        if n + 1 < len(tasks):
            following = prepare(*tasks[n + 1])
        cols = slice(g * HDIM, (g + 1) * HDIM)
        q = q_ref[rows_of(i), cols]
        gq = 0.0
        for j, at in enumerate(places_in(i)):
            low = probs_ref[i, g, rows_of(j)]
            gv = dot(low, grad, AB)
            gs = (low.astype(jnp.float32) * (gps[j] - row)).astype(jnp.bfloat16)
            gq += dot(kv_ref[buffer, 0, at, :, cols], gs, TA)
            gk = dot(gs, q, AB) * SCALE
            for kind, term in ((0, gk), (1, gv)):
                if j == 0 and i + 1 < blocks:
                    acc_ref[kind, i % 2, g] = term
                elif j == 1 and i > 0:
                    total = acc_ref[kind, at % 2, g] + term
                    out_ref[buffer, kind, at, :, cols] = total.astype(jnp.bfloat16)
                else:
                    out_ref[buffer, kind, at, :, cols] = term.astype(jnp.bfloat16)
        gq_ref[rows_of(i), cols] = (jnp.transpose(gq) * SCALE).astype(jnp.bfloat16)

    jobs = []
    for kind in range(2):
        writes = [steps > 0] * blocks
        for at in range(terms - 1, blocks - 1, -1):
            taken = False
            for to in list(range(blocks)) + list(range(at - 1, blocks - 1, -1)):
                here = (places[kind][at] == places[kind][to]) & jnp.logical_not(taken)
                taken = taken | here

                @pl.when(here)
                def _(kind=kind, at=at, to=to):
                    out_ref[buffer, kind, to] = (
                        out_ref[buffer, kind, to].astype(jnp.float32)
                        + out_ref[buffer, kind, at].astype(jnp.float32)
                    ).astype(jnp.bfloat16)

            writes.insert(blocks, jnp.logical_not(taken))
        for at in range(terms):
            jobs.append((kind, at, places[kind][at], writes[at]))

    def store(n, job, slot_h, buffer):
        kind, at, place, valid = job
        return valid, pltpu.make_async_copy(
            out_ref.at[buffer, kind, at],
            pool_ref.at[place, :, columns(slot_h)],
            sems.at[n],
        )

    for n, job in enumerate(jobs):
        valid, copy = store(n, job, jnp.maximum(h - 1, 0), 1 - buffer)
        pl.when(valid & (h > 0))(copy.wait)
    for n, job in enumerate(jobs):
        valid, copy = store(n, job, h, buffer)
        pl.when(valid)(copy.start)

    @pl.when(h == steps - 1)
    def _():
        for n, job in enumerate(jobs):
            valid, copy = store(n, job, h, buffer)
            pl.when(valid)(copy.wait)


def attention(queries, pool, gain, grad_normed, tab, lay):
    rows, columns = queries.shape
    blocks = lay.blocks
    heads = columns // HDIM
    group = 2 if heads % 2 == 0 else 1
    width = group * HDIM
    row_spec = pl.BlockSpec((rows, width), lambda h, tab: (0, h))
    gain_spec = pl.BlockSpec((1, width), lambda h, tab: (0, h))
    probs_spec = pl.BlockSpec((blocks, group, 3 * BLOCK, BLOCK), lambda h, tab: (0, h, 0, 0))
    sums_spec = pl.BlockSpec((8, rows), lambda h, tab: (0, 0))

    def pick_specs(own, picks):
        specs = [pl.BlockSpec((blocks, BLOCK, width), own)]
        for j in range(blocks + 1):
            specs.append(
                pl.BlockSpec((1, BLOCK, width), lambda h, tab, j=j: (tab[picks + j], 0, h))
            )
        return specs

    pool_specs = pick_specs(lambda h, tab: (tab[lay.device] >> 1, 0, h), lay.key_picks)
    pool_specs += pick_specs(lambda h, tab: (lay.value_own // blocks, 0, h), lay.value_picks)
    common = [row_spec] + pool_specs + [gain_spec, row_spec]
    operands = (queries,) + (pool,) * len(pool_specs) + (gain, grad_normed)

    attended, probs, sums = pl.pallas_call(
        functools.partial(forward_kernel, lay=lay, group=group),
        out_shape=(
            jax.ShapeDtypeStruct((rows, columns), jnp.float32),
            jax.ShapeDtypeStruct((blocks, heads, 3 * BLOCK, BLOCK), jnp.bfloat16),
            jax.ShapeDtypeStruct((8, rows), jnp.float32),
        ),
        grid_spec=pltpu.PrefetchScalarGridSpec(
            num_scalar_prefetch=1,
            grid=(heads // group,),
            in_specs=common,
            out_specs=(row_spec, probs_spec, sums_spec),
            scratch_shapes=[pltpu.VMEM((blocks, BLOCK, LANES), jnp.float32)],
        ),
        compiler_params=BIG,
        cost_estimate=pl.CostEstimate(
            flops=4 * rows * 3 * BLOCK * columns,
            bytes_accessed=50_000_000,
            transcendentals=rows * 3 * BLOCK * heads,
        ),
        name="attention_forward",
    )(tab, *operands)

    heads_size = lax.axis_size("head")
    sums = [sums] + [
        lax.ppermute(sums, "head", [(d, (d + k) % heads_size) for d in range(heads_size)])
        for k in range(1, heads_size)
    ]

    wide = jax.ShapeDtypeStruct((rows, columns), jnp.bfloat16)
    terms = (2, 2 * blocks + 1, BLOCK, width)
    normed, grad_q, pool = pl.pallas_call(
        functools.partial(backward_kernel, lay=lay, group=group),
        out_shape=(wide, wide, jax.ShapeDtypeStruct(pool.shape, pool.dtype)),
        grid_spec=pltpu.PrefetchScalarGridSpec(
            num_scalar_prefetch=1,
            grid=(heads // group,),
            in_specs=[row_spec, ANY, gain_spec, row_spec, row_spec, probs_spec]
            + [sums_spec] * len(sums),
            out_specs=(row_spec, row_spec, ANY),
            scratch_shapes=[
                pltpu.VMEM((blocks, BLOCK, LANES), jnp.float32),
                pltpu.VMEM((2, 2, group, BLOCK, HDIM), jnp.float32),
                pltpu.VMEM((2,) + terms, jnp.bfloat16),
                pltpu.VMEM((2,) + terms, jnp.bfloat16),
                pltpu.SemaphoreType.DMA((2 * terms[1],)),
                pltpu.SemaphoreType.DMA((2, 2 * terms[1])),
            ],
        ),
        input_output_aliases={2: 2},
        compiler_params=BIG,
        cost_estimate=pl.CostEstimate(
            flops=8 * rows * 3 * BLOCK * columns,
            bytes_accessed=70_000_000,
            transcendentals=0,
        ),
        name="attention_backward",
    )(tab, queries, pool, gain, grad_normed, attended, probs, *sums)
    return normed, grad_q, pool


def on_device(queries, key_rows, value_rows, norm_gain, sort_index, grad_normed):
    rows, columns = queries.shape
    blocks = rows // BLOCK
    lay = Layout(lax.axis_size("ctx"), blocks)
    tab, gain = routing_table(sort_index, norm_gain, lay)

    shape3 = (blocks, BLOCK, columns)
    own = (key_rows.reshape(shape3), value_rows.reshape(shape3))
    pool = gather_blocks(*own, tab, lay)

    normed, grad_q, pool = attention(queries, pool, gain, grad_normed, tab, lay)
    grad_k, grad_v = return_blocks(pool, tab, lay)
    return normed, grad_q, grad_k.reshape(rows, columns), grad_v.reshape(rows, columns)


def solution(mesh):
    in_specs = (
        P("ctx", "head"),
        P("ctx", "head"),
        P("ctx", "head"),
        P("head"),
        P(),
        P("ctx", "head"),
    )
    out_specs = (P("ctx", "head"), P("ctx", "head"), P("ctx", "head"), P("ctx", "head"))
    return jax.shard_map(
        on_device, mesh=mesh, in_specs=in_specs, out_specs=out_specs, check_vma=False
    )
```

profile of v0, /device:TPU:0, one launch (start us, length us, event | category | flops | bytes accessed | tf_op | source)
XLA Modules:
  0.0 411.9 jit_solution(11003846499795541168)
XLA Ops:
  11.8 5.4 %collective-permute-start.6 = (bf16[256,1280]{1,0:T(8,128)(2,1)}, bf16[256,1280]{1,0:T(8,128)(2,1)S(1)}, u32[]{:S(2)}, u32[]{:S(2)}) collective-permute-start(bf16[256,1280]{1,0:T(8,128)(2,1)} %get-tuple-element.260), channel_id=1, source_target_pairs={{0,8},{4,12},{8,16},{12,20},{16,24},{20,28},{1,9},{5,13},{9,17},{1... | collective-permute-start | bytes 1966088 | tf_op jit(solution)/shard_map/ppermute | solution.py:323
  24.7 6.8 %collective-permute-done.6.refs_2_ = bf16[256,1280]{1,0:T(8,128)(2,1)S(1)} collective-permute-done((bf16[256,1280]{1,0:T(8,128)(2,1)}, bf16[256,1280]{1,0:T(8,128)(2,1)S(1)}, u32[]{:S(2)}, u32[]{:S(2)}) %collective-permute-start.6) | collective-permute-done | bytes 655392 | tf_op jit(solution)/shard_map/ppermute | solution.py:323
  57.1 6.2 %collective-permute-start.15 = (bf16[256,1280]{1,0:T(8,128)(2,1)}, bf16[256,1280]{1,0:T(8,128)(2,1)S(1)}, u32[]{:S(2)}, u32[]{:S(2)}) collective-permute-start(bf16[256,1280]{1,0:T(8,128)(2,1)} %get-tuple-element.272), channel_id=1, source_target_pairs={{0,8},{4,12},{8,16},{12,20},{16,24},{20,28},{1,9},{5,13},{9,17},{1... | collective-permute-start | bytes 1966088 | tf_op jit(solution)/shard_map/ppermute | solution.py:323
  74.0 5.4 %collective-permute-start.18 = (bf16[256,1280]{1,0:T(8,128)(2,1)}, bf16[256,1280]{1,0:T(8,128)(2,1)S(1)}, u32[]{:S(2)}, u32[]{:S(2)}) collective-permute-start(bf16[256,1280]{1,0:T(8,128)(2,1)} %get-tuple-element.276), channel_id=1, source_target_pairs={{0,8},{4,12},{8,16},{12,20},{16,24},{20,28},{1,9},{5,13},{9,17},{1... | collective-permute-start | bytes 1966088 | tf_op jit(solution)/shard_map/ppermute | solution.py:323
  87.5 5.1 %collective-permute-start.21 = (bf16[256,1280]{1,0:T(8,128)(2,1)}, bf16[256,1280]{1,0:T(8,128)(2,1)S(1)}, u32[]{:S(2)}, u32[]{:S(2)}) collective-permute-start(bf16[256,1280]{1,0:T(8,128)(2,1)} %get-tuple-element.280), channel_id=1, source_target_pairs={{0,8},{4,12},{8,16},{12,20},{16,24},{20,28},{1,9},{5,13},{9,17},{1... | collective-permute-start | bytes 1966088 | tf_op jit(solution)/shard_map/ppermute | solution.py:323
  140.7 7.1 %collective-permute-done.30 = bf16[256,1280]{1,0:T(8,128)(2,1)S(1)} collective-permute-done((bf16[256,1280]{1,0:T(8,128)(2,1)}, bf16[256,1280]{1,0:T(8,128)(2,1)S(1)}, u32[]{:S(2)}, u32[]{:S(2)}) %collective-permute-start.30) | collective-permute-done | bytes 655392 | tf_op jit(solution)/shard_map/ppermute | solution.py:323
  151.8 28.9 %while.46 = (s32[]{:T(128)}, bf16[46,256,1280]{2,1,0:T(8,128)(2,1)}, bf16[256,1280]{1,0:T(8,128)(2,1)S(1)}, bf16[256,1280]{1,0:T(8,128)(2,1)S(1)}, bf16[256,1280...) while((s32[]{:T(128)}, ...), condition=%wide.region_1.2_spmd, body=%wide.region_0.1_spmd.sunk | while | flops 2 | bytes 23593188 | solution.py:399
  154.6 6.5 %collective-permute-start = (bf16[256,1280]{1,0:T(8,128)(2,1)}, bf16[256,1280]{1,0:T(8,128)(2,1)}, u32[]{:S(2)}, u32[]{:S(2)}) collective-permute-start(bf16[256,1280]{1,0:T(8,128)(2,1)} %get-tuple-element.501), channel_id=1, source_target_pairs={{0,8},{4,12},{8,16},{12,20},{16,24},{20,28},{1,9},{5,13},{9,17},{1... | collective-permute-start | bytes 1966088 | tf_op jit(solution)/shard_map/while/body/ppermute | solution.py:323
  164.5 7.1 %collective-permute-done = bf16[256,1280]{1,0:T(8,128)(2,1)} collective-permute-done((bf16[256,1280]{1,0:T(8,128)(2,1)}, bf16[256,1280]{1,0:T(8,128)(2,1)}, u32[]{:S(2)}, u32[]{:S(2)}) %collective-permute-start) | collective-permute-done | bytes 655392 | tf_op jit(solution)/shard_map/while/body/ppermute | solution.py:323
  182.4 22.8 %attention_forward.1 = (f32[1024,1280]{1,0:T(8,128)}, bf16[4,10,768,256]{3,2,1,0:T(8,128)(2,1)}, f32[8,1024]{1,0:T(8,128)}) custom-call(s32[1744]{0:T(1024)} %reshape.39.tab_ref.refs_0_.refs_1_, bf16[1024,1280]{1,0:T(8,128)(2,1)} %q_ref.1, ...), custom_call_target="tpu_custom_call" | custom-call | flops 4026531840 | bytes 50000000 | tf_op jit(solution)/shard_map/attention_forward/pallas_call | solution.py:810
  210.8 30.3 %attention_backward.1 = (bf16[1024,1280]{1,0:T(8,128)(2,1)}, bf16[1024,1280]{1,0:T(8,128)(2,1)}, bf16[46,256,1280]{2,1,0:T(8,128)(2,1)}) custom-call(s32[1744]{0:T(1024)} %reshape.39.tab_ref.refs_0_.refs_1_, bf16[1024,1280]{1,0:T(8,128)(2,1)} %q_ref.1, ...), custom_call_target="tpu_custom_call", output_to_operand_aliasing={{2}: (2, {})} | custom-call | flops 8053063680 | bytes 70000000 | tf_op jit(solution)/shard_map/attention_backward/pallas_call | solution.py:841
  242.3 25.8 %while.47 = (s32[]{:T(128)}, bf16[46,256,1280]{2,1,0:T(8,128)(2,1)}, bf16[256,1280]{1,0:T(8,128)(2,1)S(1)}, bf16[256,1280]{1,0:T(8,128)(2,1)S(1)}, bf16[256,1280...) while((s32[]{:T(128)}, ...), condition=%wide.region_3.4_spmd, body=%wide.region_2.3_spmd.sunk | while | flops 2 | bytes 25559260 | solution.py:542
  244.6 5.4 %collective-permute-start.4 = (bf16[256,1280]{1,0:T(8,128)(2,1)}, bf16[256,1280]{1,0:T(8,128)(2,1)}, u32[]{:S(2)}, u32[]{:S(2)}) collective-permute-start(bf16[256,1280]{1,0:T(8,128)(2,1)} %get-tuple-element.515), channel_id=1, source_target_pairs={{0,8},{4,12},{8,16},{12,20},{16,24},{20,28},{1,9},{5,13},{9,17},{1... | collective-permute-start | bytes 1966088 | tf_op jit(solution)/shard_map/while/body/ppermute | solution.py:323
  252.1 10.6 %collective-permute-done.3 = bf16[256,1280]{1,0:T(8,128)(2,1)} collective-permute-done((bf16[256,1280]{1,0:T(8,128)(2,1)}, bf16[256,1280]{1,0:T(8,128)(2,1)}, u32[]{:S(2)}, u32[]{:S(2)}) %collective-permute-start.3) | collective-permute-done | bytes 655392 | tf_op jit(solution)/shard_map/while/body/ppermute | solution.py:323
  278.4 6.9 %collective-permute-start.40 = (bf16[256,1280]{1,0:T(8,128)(2,1)}, bf16[256,1280]{1,0:T(8,128)(2,1)S(1)}, u32[]{:S(2)}, u32[]{:S(2)}) collective-permute-start(bf16[256,1280]{1,0:T(8,128)(2,1)} %get-tuple-element.323), channel_id=1, source_target_pairs={{0,8},{4,12},{8,16},{12,20},{16,24},{20,28},{1,9},{5,13},{9,17},{1... | collective-permute-start | bytes 1966088 | tf_op jit(solution)/shard_map/ppermute | solution.py:323
  298.3 5.6 %collective-permute-start.43 = (bf16[256,1280]{1,0:T(8,128)(2,1)}, bf16[256,1280]{1,0:T(8,128)(2,1)S(1)}, u32[]{:S(2)}, u32[]{:S(2)}) collective-permute-start(bf16[256,1280]{1,0:T(8,128)(2,1)} %get-tuple-element.327), channel_id=1, source_target_pairs={{0,8},{4,12},{8,16},{12,20},{16,24},{20,28},{1,9},{5,13},{9,17},{1... | collective-permute-start | bytes 1966088 | tf_op jit(solution)/shard_map/ppermute | solution.py:323
  310.8 7.2 %collective-permute-start.46 = (bf16[256,1280]{1,0:T(8,128)(2,1)}, bf16[256,1280]{1,0:T(8,128)(2,1)S(1)}, u32[]{:S(2)}, u32[]{:S(2)}) collective-permute-start(bf16[256,1280]{1,0:T(8,128)(2,1)} %get-tuple-element.331), channel_id=1, source_target_pairs={{0,8},{4,12},{8,16},{12,20},{16,24},{20,28},{1,9},{5,13},{9,17},{1... | collective-permute-start | bytes 1966088 | tf_op jit(solution)/shard_map/ppermute | solution.py:323
  324.7 7.8 %collective-permute-start.49 = (bf16[256,1280]{1,0:T(8,128)(2,1)}, bf16[256,1280]{1,0:T(8,128)(2,1)S(1)}, u32[]{:S(2)}, u32[]{:S(2)}) collective-permute-start(bf16[256,1280]{1,0:T(8,128)(2,1)} %get-tuple-element.335), channel_id=1, source_target_pairs={{0,8},{4,12},{8,16},{12,20},{16,24},{20,28},{1,9},{5,13},{9,17},{1... | collective-permute-start | bytes 1966088 | tf_op jit(solution)/shard_map/ppermute | solution.py:323
  338.7 8.9 %collective-permute-start.52 = (bf16[256,1280]{1,0:T(8,128)(2,1)}, bf16[256,1280]{1,0:T(8,128)(2,1)S(1)}, u32[]{:S(2)}, u32[]{:S(2)}) collective-permute-start(bf16[256,1280]{1,0:T(8,128)(2,1)} %get-tuple-element.339), channel_id=1, source_target_pairs={{0,8},{4,12},{8,16},{12,20},{16,24},{20,28},{1,9},{5,13},{9,17},{1... | collective-permute-start | bytes 1966088 | tf_op jit(solution)/shard_map/ppermute | solution.py:323
  353.9 8.8 %collective-permute-start.55 = (bf16[256,1280]{1,0:T(8,128)(2,1)}, bf16[256,1280]{1,0:T(8,128)(2,1)S(1)}, u32[]{:S(2)}, u32[]{:S(2)}) collective-permute-start(bf16[256,1280]{1,0:T(8,128)(2,1)} %get-tuple-element.343), channel_id=1, source_target_pairs={{0,8},{4,12},{8,16},{12,20},{16,24},{20,28},{1,9},{5,13},{9,17},{1... | collective-permute-start | bytes 1966088 | tf_op jit(solution)/shard_map/ppermute | solution.py:323
  368.9 7.2 %collective-permute-start.58 = (bf16[256,1280]{1,0:T(8,128)(2,1)}, bf16[256,1280]{1,0:T(8,128)(2,1)S(1)}, u32[]{:S(2)}, u32[]{:S(2)}) collective-permute-start(bf16[256,1280]{1,0:T(8,128)(2,1)} %get-tuple-element.347), channel_id=1, source_target_pairs={{0,8},{4,12},{8,16},{12,20},{16,24},{20,28},{1,9},{5,13},{9,17},{1... | collective-permute-start | bytes 1966088 | tf_op jit(solution)/shard_map/ppermute | solution.py:323
  383.8 7.2 %collective-permute-start.61 = (bf16[256,1280]{1,0:T(8,128)(2,1)}, bf16[256,1280]{1,0:T(8,128)(2,1)S(1)}, u32[]{:S(2)}, u32[]{:S(2)}) collective-permute-start(bf16[256,1280]{1,0:T(8,128)(2,1)} %get-tuple-element.350), channel_id=1, source_target_pairs={{0,8},{4,12},{8,16},{12,20},{16,24},{20,28},{1,9},{5,13},{9,17},{1... | collective-permute-start | bytes 1966088 | tf_op jit(solution)/shard_map/ppermute | solution.py:323
  392.1 8.1 %collective-permute-done.60.refs_3_ = bf16[256,1280]{1,0:T(8,128)(2,1)S(1)} collective-permute-done((bf16[256,1280]{1,0:T(8,128)(2,1)}, bf16[256,1280]{1,0:T(8,128)(2,1)S(1)}, u32[]{:S(2)}, u32[]{:S(2)}) %collective-permute-start.60) | collective-permute-done | bytes 655392 | tf_op jit(solution)/shard_map/ppermute | solution.py:323
  404.6 7.1 %return_home.1 = (bf16[4,256,1280]{2,1,0:T(8,128)(2,1)}, bf16[4,256,1280]{2,1,0:T(8,128)(2,1)}) custom-call(s32[1744]{0:T(1024)} %reshape.39.tab_ref.refs_0_.refs_1_, bf16[46,256,1280]{2,1,0:T(8,128)(2,1)} %get-tuple-element.345.pool_ref, bf16[256,1280]{1,0:T(8,128)(2,1)} %copy-done, bf16[256,1280]{1,0:T(8,128)(2,1)} %copy-done.1, ...), custom_call_target="tpu_custom_call" | custom-call | bytes 19660800 | tf_op jit(solution)/shard_map/return_home/pallas_call | solution.py:550
  (259 shorter events, 214.6 us)
Async XLA Ops:
  17.2 23.5 %collective-permute-start.7 = (bf16[256,1280]{1,0:T(8,128)(2,1)}, bf16[256,1280]{1,0:T(8,128)(2,1)S(1)}, u32[]{:S(2)}, u32[]{:S(2)}) collective-permute-start(bf16[256,1280]{1,0:T(8,128)(2,1)} %get-tuple-element.261), channel_id=1, source_target_pairs={{8,0},{12,4},{16,8},{20,12},{24,16},{28,20},{9,1},{13,5},{17,9},{2... | collective-permute-start | bytes 1966088 | tf_op jit(solution)/shard_map/ppermute | solution.py:323
  18.5 22.2 %collective-permute-start.8 = (bf16[256,1280]{1,0:T(8,128)(2,1)}, bf16[256,1280]{1,0:T(8,128)(2,1)S(1)}, u32[]{:S(2)}, u32[]{:S(2)}) collective-permute-start(bf16[256,1280]{1,0:T(8,128)(2,1)} %get-tuple-element.262), channel_id=1, source_target_pairs={{0,4},{4,0},{8,12},{12,8},{16,20},{20,16},{24,28},{28,24},{1,5},{5... | collective-permute-start | bytes 1966088 | tf_op jit(solution)/shard_map/ppermute | solution.py:323
  23.3 28.4 %collective-permute-start.10 = (bf16[256,1280]{1,0:T(8,128)(2,1)}, bf16[256,1280]{1,0:T(8,128)(2,1)S(1)}, u32[]{:S(2)}, u32[]{:S(2)}) collective-permute-start(bf16[256,1280]{1,0:T(8,128)(2,1)} %get-tuple-element.265), channel_id=1, source_target_pairs={{8,0},{12,4},{16,8},{20,12},{24,16},{28,20},{9,1},{13,5},{17,9},{2... | collective-permute-start | bytes 1966088 | tf_op jit(solution)/shard_map/ppermute | solution.py:323
  24.6 28.2 %collective-permute-start.11 = (bf16[256,1280]{1,0:T(8,128)(2,1)}, bf16[256,1280]{1,0:T(8,128)(2,1)S(1)}, u32[]{:S(2)}, u32[]{:S(2)}) collective-permute-start(bf16[256,1280]{1,0:T(8,128)(2,1)} %get-tuple-element.266), channel_id=1, source_target_pairs={{0,4},{4,0},{8,12},{12,8},{16,20},{20,16},{24,28},{28,24},{1,5},{5... | collective-permute-start | bytes 1966088 | tf_op jit(solution)/shard_map/ppermute | solution.py:323
  31.5 21.4 %collective-permute-start.9 = (bf16[256,1280]{1,0:T(8,128)(2,1)}, bf16[256,1280]{1,0:T(8,128)(2,1)S(1)}, u32[]{:S(2)}, u32[]{:S(2)}) collective-permute-start(bf16[256,1280]{1,0:T(8,128)(2,1)} %get-tuple-element.264), channel_id=1, source_target_pairs={{0,8},{4,12},{8,16},{12,20},{16,24},{20,28},{1,9},{5,13},{9,17},{1... | collective-permute-start | bytes 1966088 | tf_op jit(solution)/shard_map/ppermute | solution.py:323
  57.1 23.5 %collective-permute-start.15 = (bf16[256,1280]{1,0:T(8,128)(2,1)}, bf16[256,1280]{1,0:T(8,128)(2,1)S(1)}, u32[]{:S(2)}, u32[]{:S(2)}) collective-permute-start(bf16[256,1280]{1,0:T(8,128)(2,1)} %get-tuple-element.272), channel_id=1, source_target_pairs={{0,8},{4,12},{8,16},{12,20},{16,24},{20,28},{1,9},{5,13},{9,17},{1... | collective-permute-start | bytes 1966088 | tf_op jit(solution)/shard_map/ppermute | solution.py:323
  63.3 20.1 %collective-permute-start.16 = (bf16[256,1280]{1,0:T(8,128)(2,1)}, bf16[256,1280]{1,0:T(8,128)(2,1)S(1)}, u32[]{:S(2)}, u32[]{:S(2)}) collective-permute-start(bf16[256,1280]{1,0:T(8,128)(2,1)} %get-tuple-element.273), channel_id=1, source_target_pairs={{8,0},{12,4},{16,8},{20,12},{24,16},{28,20},{9,1},{13,5},{17,9},{2... | collective-permute-start | bytes 1966088 | tf_op jit(solution)/shard_map/ppermute | solution.py:323
  74.0 20.5 %collective-permute-start.18 = (bf16[256,1280]{1,0:T(8,128)(2,1)}, bf16[256,1280]{1,0:T(8,128)(2,1)S(1)}, u32[]{:S(2)}, u32[]{:S(2)}) collective-permute-start(bf16[256,1280]{1,0:T(8,128)(2,1)} %get-tuple-element.276), channel_id=1, source_target_pairs={{0,8},{4,12},{8,16},{12,20},{16,24},{20,28},{1,9},{5,13},{9,17},{1... | collective-permute-start | bytes 1966088 | tf_op jit(solution)/shard_map/ppermute | solution.py:323
  87.5 21.0 %collective-permute-start.21 = (bf16[256,1280]{1,0:T(8,128)(2,1)}, bf16[256,1280]{1,0:T(8,128)(2,1)S(1)}, u32[]{:S(2)}, u32[]{:S(2)}) collective-permute-start(bf16[256,1280]{1,0:T(8,128)(2,1)} %get-tuple-element.280), channel_id=1, source_target_pairs={{0,8},{4,12},{8,16},{12,20},{16,24},{20,28},{1,9},{5,13},{9,17},{1... | collective-permute-start | bytes 1966088 | tf_op jit(solution)/shard_map/ppermute | solution.py:323
  116.4 20.2 %collective-permute-start.27 = (bf16[256,1280]{1,0:T(8,128)(2,1)}, bf16[256,1280]{1,0:T(8,128)(2,1)S(1)}, u32[]{:S(2)}, u32[]{:S(2)}) collective-permute-start(bf16[256,1280]{1,0:T(8,128)(2,1)} %get-tuple-element.288), channel_id=1, source_target_pairs={{0,8},{4,12},{8,16},{12,20},{16,24},{20,28},{1,9},{5,13},{9,17},{1... | collective-permute-start | bytes 1966088 | tf_op jit(solution)/shard_map/ppermute | solution.py:323
  277.1 26.8 %collective-permute-start.39 = (bf16[256,1280]{1,0:T(8,128)(2,1)}, bf16[256,1280]{1,0:T(8,128)(2,1)S(1)}, u32[]{:S(2)}, u32[]{:S(2)}) collective-permute-start(bf16[256,1280]{1,0:T(8,128)(2,1)} %get-tuple-element.322), channel_id=1, source_target_pairs={{8,0},{12,4},{16,8},{20,12},{24,16},{28,20},{9,1},{13,5},{17,9},{2... | collective-permute-start | bytes 1966088 | tf_op jit(solution)/shard_map/ppermute | solution.py:323
  278.4 25.7 %collective-permute-start.40 = (bf16[256,1280]{1,0:T(8,128)(2,1)}, bf16[256,1280]{1,0:T(8,128)(2,1)S(1)}, u32[]{:S(2)}, u32[]{:S(2)}) collective-permute-start(bf16[256,1280]{1,0:T(8,128)(2,1)} %get-tuple-element.323), channel_id=1, source_target_pairs={{0,8},{4,12},{8,16},{12,20},{16,24},{20,28},{1,9},{5,13},{9,17},{1... | collective-permute-start | bytes 1966088 | tf_op jit(solution)/shard_map/ppermute | solution.py:323
  297.0 21.0 %collective-permute-start.42 = (bf16[256,1280]{1,0:T(8,128)(2,1)}, bf16[256,1280]{1,0:T(8,128)(2,1)S(1)}, u32[]{:S(2)}, u32[]{:S(2)}) collective-permute-start(bf16[256,1280]{1,0:T(8,128)(2,1)} %get-tuple-element.326), channel_id=1, source_target_pairs={{8,0},{12,4},{16,8},{20,12},{24,16},{28,20},{9,1},{13,5},{17,9},{2... | collective-permute-start | bytes 1966088 | tf_op jit(solution)/shard_map/ppermute | solution.py:323
  298.3 20.4 %collective-permute-start.43 = (bf16[256,1280]{1,0:T(8,128)(2,1)}, bf16[256,1280]{1,0:T(8,128)(2,1)S(1)}, u32[]{:S(2)}, u32[]{:S(2)}) collective-permute-start(bf16[256,1280]{1,0:T(8,128)(2,1)} %get-tuple-element.327), channel_id=1, source_target_pairs={{0,8},{4,12},{8,16},{12,20},{16,24},{20,28},{1,9},{5,13},{9,17},{1... | collective-permute-start | bytes 1966088 | tf_op jit(solution)/shard_map/ppermute | solution.py:323
  309.5 23.0 %collective-permute-start.45 = (bf16[256,1280]{1,0:T(8,128)(2,1)}, bf16[256,1280]{1,0:T(8,128)(2,1)S(1)}, u32[]{:S(2)}, u32[]{:S(2)}) collective-permute-start(bf16[256,1280]{1,0:T(8,128)(2,1)} %get-tuple-element.330), channel_id=1, source_target_pairs={{8,0},{12,4},{16,8},{20,12},{24,16},{28,20},{9,1},{13,5},{17,9},{2... | collective-permute-start | bytes 1966088 | tf_op jit(solution)/shard_map/ppermute | solution.py:323
  310.8 22.6 %collective-permute-start.46 = (bf16[256,1280]{1,0:T(8,128)(2,1)}, bf16[256,1280]{1,0:T(8,128)(2,1)S(1)}, u32[]{:S(2)}, u32[]{:S(2)}) collective-permute-start(bf16[256,1280]{1,0:T(8,128)(2,1)} %get-tuple-element.331), channel_id=1, source_target_pairs={{0,8},{4,12},{8,16},{12,20},{16,24},{20,28},{1,9},{5,13},{9,17},{1... | collective-permute-start | bytes 1966088 | tf_op jit(solution)/shard_map/ppermute | solution.py:323
  323.4 24.2 %collective-permute-start.48 = (bf16[256,1280]{1,0:T(8,128)(2,1)}, bf16[256,1280]{1,0:T(8,128)(2,1)S(1)}, u32[]{:S(2)}, u32[]{:S(2)}) collective-permute-start(bf16[256,1280]{1,0:T(8,128)(2,1)} %get-tuple-element.334), channel_id=1, source_target_pairs={{8,0},{12,4},{16,8},{20,12},{24,16},{28,20},{9,1},{13,5},{17,9},{2... | collective-permute-start | bytes 1966088 | tf_op jit(solution)/shard_map/ppermute | solution.py:323
  324.7 23.0 %collective-permute-start.49 = (bf16[256,1280]{1,0:T(8,128)(2,1)}, bf16[256,1280]{1,0:T(8,128)(2,1)S(1)}, u32[]{:S(2)}, u32[]{:S(2)}) collective-permute-start(bf16[256,1280]{1,0:T(8,128)(2,1)} %get-tuple-element.335), channel_id=1, source_target_pairs={{0,8},{4,12},{8,16},{12,20},{16,24},{20,28},{1,9},{5,13},{9,17},{1... | collective-permute-start | bytes 1966088 | tf_op jit(solution)/shard_map/ppermute | solution.py:323
  337.4 25.2 %collective-permute-start.51 = (bf16[256,1280]{1,0:T(8,128)(2,1)}, bf16[256,1280]{1,0:T(8,128)(2,1)S(1)}, u32[]{:S(2)}, u32[]{:S(2)}) collective-permute-start(bf16[256,1280]{1,0:T(8,128)(2,1)} %get-tuple-element.338), channel_id=1, source_target_pairs={{8,0},{12,4},{16,8},{20,12},{24,16},{28,20},{9,1},{13,5},{17,9},{2... | collective-permute-start | bytes 1966088 | tf_op jit(solution)/shard_map/ppermute | solution.py:323
  338.7 24.0 %collective-permute-start.52 = (bf16[256,1280]{1,0:T(8,128)(2,1)}, bf16[256,1280]{1,0:T(8,128)(2,1)S(1)}, u32[]{:S(2)}, u32[]{:S(2)}) collective-permute-start(bf16[256,1280]{1,0:T(8,128)(2,1)} %get-tuple-element.339), channel_id=1, source_target_pairs={{0,8},{4,12},{8,16},{12,20},{16,24},{20,28},{1,9},{5,13},{9,17},{1... | collective-permute-start | bytes 1966088 | tf_op jit(solution)/shard_map/ppermute | solution.py:323
  352.6 23.6 %collective-permute-start.54 = (bf16[256,1280]{1,0:T(8,128)(2,1)}, bf16[256,1280]{1,0:T(8,128)(2,1)S(1)}, u32[]{:S(2)}, u32[]{:S(2)}) collective-permute-start(bf16[256,1280]{1,0:T(8,128)(2,1)} %get-tuple-element.342), channel_id=1, source_target_pairs={{8,0},{12,4},{16,8},{20,12},{24,16},{28,20},{9,1},{13,5},{17,9},{2... | collective-permute-start | bytes 1966088 | tf_op jit(solution)/shard_map/ppermute | solution.py:323
  353.9 22.4 %collective-permute-start.55 = (bf16[256,1280]{1,0:T(8,128)(2,1)}, bf16[256,1280]{1,0:T(8,128)(2,1)S(1)}, u32[]{:S(2)}, u32[]{:S(2)}) collective-permute-start(bf16[256,1280]{1,0:T(8,128)(2,1)} %get-tuple-element.343), channel_id=1, source_target_pairs={{0,8},{4,12},{8,16},{12,20},{16,24},{20,28},{1,9},{5,13},{9,17},{1... | collective-permute-start | bytes 1966088 | tf_op jit(solution)/shard_map/ppermute | solution.py:323
  367.6 23.4 %collective-permute-start.57 = (bf16[256,1280]{1,0:T(8,128)(2,1)}, bf16[256,1280]{1,0:T(8,128)(2,1)S(1)}, u32[]{:S(2)}, u32[]{:S(2)}) collective-permute-start(bf16[256,1280]{1,0:T(8,128)(2,1)} %get-tuple-element.346), channel_id=1, source_target_pairs={{8,0},{12,4},{16,8},{20,12},{24,16},{28,20},{9,1},{13,5},{17,9},{2... | collective-permute-start | bytes 1966088 | tf_op jit(solution)/shard_map/ppermute | solution.py:323
  368.9 22.2 %collective-permute-start.58 = (bf16[256,1280]{1,0:T(8,128)(2,1)}, bf16[256,1280]{1,0:T(8,128)(2,1)S(1)}, u32[]{:S(2)}, u32[]{:S(2)}) collective-permute-start(bf16[256,1280]{1,0:T(8,128)(2,1)} %get-tuple-element.347), channel_id=1, source_target_pairs={{0,8},{4,12},{8,16},{12,20},{16,24},{20,28},{1,9},{5,13},{9,17},{1... | collective-permute-start | bytes 1966088 | tf_op jit(solution)/shard_map/ppermute | solution.py:323
  (90 other events, 759.8 us)
where the time goes:
time: 417 us; the launch traced here: 412 us
  starting transfers between devices  162 us (39%)
  Pallas kernels  128 us (31%)
  waiting for transfers between devices  85 us (20%)
  local copies, waits for them, and re-layouts  32.5 us (8%)
    ppermute x60, starting transfers between devices, send_all(): return tuple((lax.ppermute(s, 'ctx', p) for s, p in zip(sends, perms)))  159 us
    ppermute x60, waiting for transfers between devices, send_all(): return tuple((lax.ppermute(s, 'ctx', p) for s, p in zip(sends, perms)))  85 us
    pallas_call x1, Pallas kernels, attention(): pl.pallas_call(functools.partial(backward_kernel, lay=lay, group=group),...  30.3 us
    pallas_call x10, Pallas kernels, step(): pool, *sends = numbered(back_kernel, t, call)(tab, pool, *got)  27 us
    pallas_call x8, Pallas kernels, step(): pool, *sends = numbered(step_kernel, t, call)(tab, pool, *got)  23.6 us
    pallas_call x1, Pallas kernels, attention(): pl.pallas_call(functools.partial(forward_kernel, lay=lay, group=group), o...  22.8 us
    unnamed x102, local copies, waits for them, and re-layouts  16.1 us
    while x12, local copies, waits for them, and re-layouts  8.38 us
  transfers between devices with their start and end apart: 63, of which 29 were waited for; matrix products, arithmetic and copies ran while one was open for 2% of the time, Pallas kernels for 14%

commit v1 on v0

--- a/solution.py
+++ b/solution.py
@@ -303,20 +303,46 @@
     copies(stores, sems)
 
 
-def close_kernel(*refs, slot, back):
+def close_kernel(*refs, slot):
     t, refs = slot_and_rest(slot, refs)
     tab_ref, _, in_up, in_down, in_over, pool_ref, held_ref, sems = refs
     loads, stores = [], []
     for k, got in enumerate((in_up, in_down, in_over)):
-        code = entry(tab_ref, t - back, 3 + k)
+        code = entry(tab_ref, t, 3 + k)
         loads.append((code >= 0, got, held_ref.at[k]))
         stores.append((code >= 0, held_ref.at[k], pool_ref.at[place_of(code)]))
     copies(loads, sems)
     copies(stores, sems)
 
 
+def take_kernel(*refs, slot, first):
+    t, refs = slot_and_rest(slot, refs)
+    tab_ref, pool_ref, up_ref, down_ref, over_ref, held_ref, sems = refs
+    loads, stores = [], []
+    for k, out in enumerate((up_ref, down_ref, over_ref)):
+        code = entry(tab_ref, t, first + k)
+        loads.append((code >= 0, pool_ref.at[place_of(code)], held_ref.at[k]))
+        stores.append((code >= 0, held_ref.at[k], out))
+    copies(loads, sems)
+    copies(stores, sems)
+
+
 def traffic(byte_count):
     return pl.CostEstimate(flops=0, bytes_accessed=byte_count, transcendentals=0)
+
+
+def take(t, tab, pool, first):
+    one = jax.ShapeDtypeStruct(pool.shape[1:], pool.dtype)
+    call = dict(
+        out_shape=(one,) * 3,
+        in_specs=[SMEM, ANY],
+        out_specs=(ANY,) * 3,
+        scratch_shapes=[pltpu.VMEM((3,) + one.shape, one.dtype), pltpu.SemaphoreType.DMA((3,))],
+        cost_estimate=traffic(12 * math.prod(one.shape)),
+        name="take_step",
+        in_place=False,
+    )
+    return numbered(functools.partial(take_kernel, first=first), t, call)(tab, pool)
 
 
 def send_all(sends, perms):
@@ -331,7 +357,7 @@
         pl.pallas_call(
             functools.partial(kernel, slot=t if known else None),
             in_specs=specs + call.pop("in_specs"),
-            input_output_aliases={1 + len(extra): 0},
+            input_output_aliases={1 + len(extra): 0} if call.pop("in_place", True) else {},
             compiler_params=MOVE,
             **call,
         ),
@@ -339,7 +365,7 @@
     )
 
 
-def gather_blocks(keys, values, tab, lay):
+def gather_blocks(keys, values, tab, total, lay):
     one = jax.ShapeDtypeStruct(keys.shape[1:], keys.dtype)
     pool_shape = jax.ShapeDtypeStruct((lay.places,) + one.shape, one.dtype)
     size = 2 * math.prod(one.shape)
@@ -391,17 +417,7 @@
         pool, latest = step(t, pool, older)
         older, newer = newer, latest
 
-    def body(state):
-        t, pool, older, newer = state
-        pool, latest = step(t, pool, older)
-        return t + 1, pool, newer, latest
-
-    t, pool, older, newer = lax.while_loop(
-        lambda state: state[0] < tab[lay.total],
-        body,
-        (jnp.int32(STATIC_SLOTS), pool, older, newer),
-    )
-    for back, got in ((2, older), (1, newer)):
+    def close(t, pool, got):
         call = dict(
             out_shape=pool_shape,
             in_specs=[SMEM] + [ANY] * 4,
@@ -410,8 +426,19 @@
             cost_estimate=traffic(size * 6),
             name="gather_close",
         )
-        pool = numbered(functools.partial(close_kernel, back=back), t, call)(tab, pool, *got)
-    return pool
+        return numbered(close_kernel, t, call)(tab, pool, *got)
+
+    pool = close(STATIC_SLOTS - 2, pool, older)
+    pool = close(STATIC_SLOTS - 1, pool, newer)
+
+    def body(state):
+        t, end, pool = state
+        got = send_all(take(t, tab, pool, 0), perms)
+        return t + 1, end, close(t, pool, got)
+
+    return lax.while_loop(
+        lambda state: state[0] < state[1], body, (jnp.int32(STATIC_SLOTS), total, pool)
+    )[2]
 
 
 def add(target_ref, to, source_ref, at):
@@ -422,11 +449,19 @@
 
 def back_kernel(*refs, slot):
     t, refs = slot_and_rest(slot, refs)
-    (
-        tab_ref, _, in_up, in_down, in_over, pool_ref, up_ref, down_ref, over_ref,
-        held_ref, got_ref, sems,
-    ) = refs
-    codes = [entry(tab_ref, t + 2, k) for k in range(3)]
+    tab_ref, _, in_up, in_down, in_over, pool_ref, up_ref, down_ref, over_ref = refs[:9]
+    takes = [(entry(tab_ref, t, 3 + k), out) for k, out in enumerate((up_ref, down_ref, over_ref))]
+    fold(tab_ref, t + 2, (in_up, in_down, in_over), takes, pool_ref, *refs[9:])
+
+
+def add_kernel(*refs, slot):
+    t, refs = slot_and_rest(slot, refs)
+    tab_ref, _, in_up, in_down, in_over, pool_ref = refs[:6]
+    fold(tab_ref, t, (in_up, in_down, in_over), [], pool_ref, *refs[6:])
+
+
+def fold(tab_ref, t, arrived, takes, pool_ref, held_ref, got_ref, sems):
+    codes = [entry(tab_ref, t, k) for k in range(3)]
     places = [place_of(c) for c in codes]
     valid = [c >= 0 for c in codes]
     fresh = [c >= FIRST for c in codes]
@@ -438,22 +473,19 @@
         valid[1] & jnp.logical_not(same_10),
         valid[2] & jnp.logical_not(same_20 | same_21),
     ]
-    loads = [
-        (v, got, got_ref.at[k]) for k, (v, got) in enumerate(zip(valid, (in_up, in_down, in_over)))
-    ]
+    loads = [(v, got, got_ref.at[k]) for k, (v, got) in enumerate(zip(valid, arrived))]
     loads += [
         (a & jnp.logical_not(f), pool_ref.at[p], held_ref.at[k])
         for k, (a, f, p) in enumerate(zip(alone, fresh, places))
     ]
     stores = []
     leaves = [False] * 3
-    for k, out in enumerate((up_ref, down_ref, over_ref)):
-        code = entry(tab_ref, t, 3 + k)
-        takes = code >= 0
+    for k, (code, out) in enumerate(takes):
+        leaving = code >= 0
         place = place_of(code)
-        found, at = match(place, takes, places, alone)
-        loads.append((takes & jnp.logical_not(found), pool_ref.at[place], held_ref.at[3 + k]))
-        stores.append((takes, held_ref.at[jnp.where(found, at, 3 + k)], out))
+        found, at = match(place, leaving, places, alone)
+        loads.append((leaving & jnp.logical_not(found), pool_ref.at[place], held_ref.at[3 + k]))
+        stores.append((leaving, held_ref.at[jnp.where(found, at, 3 + k)], out))
         leaves = [leave | (found & (at == n)) for n, leave in enumerate(leaves)]
     copies(loads, sems)
     for k in range(3):
@@ -509,7 +541,7 @@
     copies(stores, sems)
 
 
-def return_blocks(pool, tab, lay):
+def return_blocks(pool, tab, total, lay):
     one = jax.ShapeDtypeStruct(pool.shape[1:], pool.dtype)
     pool_shape = jax.ShapeDtypeStruct(pool.shape, pool.dtype)
     own_shape = jax.ShapeDtypeStruct((lay.blocks,) + one.shape, one.dtype)
@@ -517,16 +549,18 @@
     up, down, over = routes(lay.ctx_size)
     perms = ([(b, a) for a, b in up], [(b, a) for a, b in down], over)
 
+    scratch = [
+        pltpu.VMEM((6,) + one.shape, one.dtype),
+        pltpu.VMEM((3,) + one.shape, one.dtype),
+        pltpu.SemaphoreType.DMA((9,)),
+    ]
+
     def step(t, pool, got):
         call = dict(
             out_shape=(pool_shape, one, one, one),
             in_specs=[SMEM] + [ANY] * 4,
             out_specs=(ANY,) * 4,
-            scratch_shapes=[
-                pltpu.VMEM((6,) + one.shape, one.dtype),
-                pltpu.VMEM((3,) + one.shape, one.dtype),
-                pltpu.SemaphoreType.DMA((9,)),
-            ],
+            scratch_shapes=scratch,
             cost_estimate=traffic(size * 15),
             name="return_step",
         )
@@ -534,17 +568,22 @@
         return pool, send_all(sends, perms)
 
     def body(state):
-        t, pool, older, newer = state
-        pool, latest = step(t, pool, older)
-        return t - 1, pool, newer, latest
-
-    nothing = (jnp.zeros(one.shape, one.dtype),) * 3
-    _, pool, older, newer = lax.while_loop(
-        lambda state: state[0] >= STATIC_SLOTS,
-        body,
-        (tab[lay.total] - 1, pool, nothing, nothing),
-    )
-    for t in range(STATIC_SLOTS - 1, -1, -1):
+        t, pool = state
+        got = send_all(take(t, tab, pool, 3), perms)
+        call = dict(
+            out_shape=pool_shape,
+            in_specs=[SMEM] + [ANY] * 4,
+            out_specs=ANY,
+            scratch_shapes=scratch,
+            cost_estimate=traffic(size * 9),
+            name="return_add",
+        )
+        return t - 1, numbered(add_kernel, t, call)(tab, pool, *got)
+
+    _, pool = lax.while_loop(lambda state: state[0] >= STATIC_SLOTS, body, (total - 1, pool))
+    older = send_all(take(STATIC_SLOTS - 1, tab, pool, 3), perms)
+    newer = send_all(take(STATIC_SLOTS - 2, tab, pool, 3), perms)
+    for t in range(STATIC_SLOTS - 3, -1, -1):
         pool, latest = step(t, pool, older)
         older, newer = newer, latest
     return pl.pallas_call(
@@ -876,10 +915,11 @@
 
     shape3 = (blocks, BLOCK, columns)
     own = (key_rows.reshape(shape3), value_rows.reshape(shape3))
-    pool = gather_blocks(*own, tab, lay)
+    total = tab[lay.total]
+    pool = gather_blocks(*own, tab, total, lay)
 
     normed, grad_q, pool = attention(queries, pool, gain, grad_normed, tab, lay)
-    grad_k, grad_v = return_blocks(pool, tab, lay)
+    grad_k, grad_v = return_blocks(pool, tab, total, lay)
     return normed, grad_q, grad_k.reshape(rows, columns), grad_v.reshape(rows, columns)
 
 

time: 417 us -> 355 us (0.85)
  starting transfers between devices: 162 us -> 143 us
  Pallas kernels: 128 us -> 112 us
  local copies, waits for them, and re-layouts: 32.5 us -> 20.5 us
  waiting for transfers between devices: 85 us -> 73.2 us
    ppermute x60 -> x54, starting transfers between devices: 159 us -> 141 us  [send_all(): return tuple((lax.ppermute(s, 'ctx', p) for s, p in zip(sends, perms)))]
    ppermute x60 -> x54, waiting for transfers between devices: 85 us -> 70.5 us  [send_all(): return tuple((lax.ppermute(s, 'ctx', p) for s, p in zip(sends, perms)))]
    pallas_call x10 -> x7, Pallas kernels: 27 us -> 18 us  [step(): pool, *sends = numbered(back_kernel, t, call)(tab, pool, *got)]
    while x12 -> x0, local copies, waits for them, and re-layouts: 8.38 us -> none
    pallas_call x8 -> x7, Pallas kernels: 23.6 us -> 17.1 us  [step(): pool, *sends = numbered(step_kernel, t, call)(tab, pool, *got)]
    unnamed x102 -> x112, local copies, waits for them, and re-layouts: 16.1 us -> 17.2 us
  transfers between devices with their start and end apart: 63 -> 57, of which waited for: 29 -> 27; matrix products, arithmetic and copies ran while one was open for 2% -> 0% of each run, Pallas kernels for 14% -> 12%
where the time goes in v1:
time: 355 us; the launch traced here: 353 us
  starting transfers between devices  143 us (40%)
  Pallas kernels  112 us (32%)
  waiting for transfers between devices  73.2 us (21%)
  local copies, waits for them, and re-layouts  20.5 us (6%)
    ppermute x54, starting transfers between devices, send_all(): return tuple((lax.ppermute(s, 'ctx', p) for s, p in zip(sends, perms)))  141 us
    ppermute x54, waiting for transfers between devices, send_all(): return tuple((lax.ppermute(s, 'ctx', p) for s, p in zip(sends, perms)))  70.5 us
    pallas_call x1, Pallas kernels, attention(): pl.pallas_call(functools.partial(backward_kernel, lay=lay, group=group),...  30.4 us
    pallas_call x1, Pallas kernels, attention(): pl.pallas_call(functools.partial(forward_kernel, lay=lay, group=group), o...  22.9 us
    pallas_call x7, Pallas kernels, step(): pool, *sends = numbered(back_kernel, t, call)(tab, pool, *got)  18 us
    unnamed x112, local copies, waits for them, and re-layouts  17.2 us
    pallas_call x7, Pallas kernels, step(): pool, *sends = numbered(step_kernel, t, call)(tab, pool, *got)  17.1 us
  transfers between devices with their start and end apart: 57, of which 27 were waited for; matrix products, arithmetic and copies ran while one was open for 0% of the time, Pallas kernels for 12%

profile of v1, /device:TPU:0, one launch (start us, length us, event | category | flops | bytes accessed | tf_op | source)
XLA Modules:
  0.0 352.9 jit_solution(1077895099623651567)
XLA Ops:
  10.9 5.0 %collective-permute-start.6 = (bf16[256,1280]{1,0:T(8,128)(2,1)}, bf16[256,1280]{1,0:T(8,128)(2,1)S(1)}, u32[]{:S(2)}, u32[]{:S(2)}) collective-permute-start(bf16[256,1280]{1,0:T(8,128)(2,1)} %get-tuple-element.150), channel_id=1, source_target_pairs={{0,8},{4,12},{8,16},{12,20},{16,24},{20,28},{1,9},{5,13},{9,17},{1... | collective-permute-start | bytes 1966088 | tf_op jit(solution)/shard_map/ppermute | solution.py:349
  21.4 5.0 %collective-permute-start.9 = (bf16[256,1280]{1,0:T(8,128)(2,1)}, bf16[256,1280]{1,0:T(8,128)(2,1)S(1)}, u32[]{:S(2)}, u32[]{:S(2)}) collective-permute-start(bf16[256,1280]{1,0:T(8,128)(2,1)} %get-tuple-element.154), channel_id=1, source_target_pairs={{0,8},{4,12},{8,16},{12,20},{16,24},{20,28},{1,9},{5,13},{9,17},{1... | collective-permute-start | bytes 1966088 | tf_op jit(solution)/shard_map/ppermute | solution.py:349
  32.8 4.8 %gather_fill.1.refs_1_ = bf16[46,256,1280]{2,1,0:T(8,128)(2,1)} custom-call(s32[1744]{0:T(1024)S(1)} %reshape.35.tab_ref.refs_0_, bf16[4,256,1280]{2,1,0:T(8,128)(2,1)} %bitcast.13, bf16[4,256,1280]{2,1,0:T(8,128)(2,1)} %bitcast.16), custom_call_target="tpu_custom_call" | custom-call | bytes 10485760 | tf_op jit(solution)/shard_map/gather_fill/pallas_call | solution.py:390
  42.5 4.6 %collective-permute-start.12 = (bf16[256,1280]{1,0:T(8,128)(2,1)}, bf16[256,1280]{1,0:T(8,128)(2,1)S(1)}, u32[]{:S(2)}, u32[]{:S(2)}) collective-permute-start(bf16[256,1280]{1,0:T(8,128)(2,1)} %get-tuple-element.158), channel_id=1, source_target_pairs={{0,8},{4,12},{8,16},{12,20},{16,24},{20,28},{1,9},{5,13},{9,17},{1... | collective-permute-start | bytes 1966088 | tf_op jit(solution)/shard_map/ppermute | solution.py:349
  62.9 4.6 %collective-permute-done.13.refs_3_ = bf16[256,1280]{1,0:T(8,128)(2,1)S(1)} collective-permute-done((bf16[256,1280]{1,0:T(8,128)(2,1)}, bf16[256,1280]{1,0:T(8,128)(2,1)S(1)}, u32[]{:S(2)}, u32[]{:S(2)}) %collective-permute-start.13) | collective-permute-done | bytes 655392 | tf_op jit(solution)/shard_map/ppermute | solution.py:349
  71.4 5.4 %collective-permute-start.18 = (bf16[256,1280]{1,0:T(8,128)(2,1)}, bf16[256,1280]{1,0:T(8,128)(2,1)S(1)}, u32[]{:S(2)}, u32[]{:S(2)}) collective-permute-start(bf16[256,1280]{1,0:T(8,128)(2,1)} %get-tuple-element.166), channel_id=1, source_target_pairs={{0,8},{4,12},{8,16},{12,20},{16,24},{20,28},{1,9},{5,13},{9,17},{1... | collective-permute-start | bytes 1966088 | tf_op jit(solution)/shard_map/ppermute | solution.py:349
  83.4 6.5 %collective-permute-start.21 = (bf16[256,1280]{1,0:T(8,128)(2,1)}, bf16[256,1280]{1,0:T(8,128)(2,1)S(1)}, u32[]{:S(2)}, u32[]{:S(2)}) collective-permute-start(bf16[256,1280]{1,0:T(8,128)(2,1)} %get-tuple-element.170), channel_id=1, source_target_pairs={{0,8},{4,12},{8,16},{12,20},{16,24},{20,28},{1,9},{5,13},{9,17},{1... | collective-permute-start | bytes 1966088 | tf_op jit(solution)/shard_map/ppermute | solution.py:349
  91.6 5.0 %collective-permute-done.19.refs_3_ = bf16[256,1280]{1,0:T(8,128)(2,1)S(1)} collective-permute-done((bf16[256,1280]{1,0:T(8,128)(2,1)}, bf16[256,1280]{1,0:T(8,128)(2,1)S(1)}, u32[]{:S(2)}, u32[]{:S(2)}) %collective-permute-start.19) | collective-permute-done | bytes 655392 | tf_op jit(solution)/shard_map/ppermute | solution.py:349
  112.5 6.0 %collective-permute-start.27 = (bf16[256,1280]{1,0:T(8,128)(2,1)}, bf16[256,1280]{1,0:T(8,128)(2,1)S(1)}, u32[]{:S(2)}, u32[]{:S(2)}) collective-permute-start(bf16[256,1280]{1,0:T(8,128)(2,1)} %get-tuple-element.178), channel_id=1, source_target_pairs={{0,8},{4,12},{8,16},{12,20},{16,24},{20,28},{1,9},{5,13},{9,17},{1... | collective-permute-start | bytes 1966088 | tf_op jit(solution)/shard_map/ppermute | solution.py:349
  120.3 4.7 %collective-permute-done.25.refs_3_ = bf16[256,1280]{1,0:T(8,128)(2,1)S(1)} collective-permute-done((bf16[256,1280]{1,0:T(8,128)(2,1)}, bf16[256,1280]{1,0:T(8,128)(2,1)S(1)}, u32[]{:S(2)}, u32[]{:S(2)}) %collective-permute-start.25) | collective-permute-done | bytes 655392 | tf_op jit(solution)/shard_map/ppermute | solution.py:349
  143.4 4.9 %collective-permute-done.31.refs_3_ = bf16[256,1280]{1,0:T(8,128)(2,1)S(1)} collective-permute-done((bf16[256,1280]{1,0:T(8,128)(2,1)}, bf16[256,1280]{1,0:T(8,128)(2,1)S(1)}, u32[]{:S(2)}, u32[]{:S(2)}) %collective-permute-start.31) | collective-permute-done | bytes 655392 | tf_op jit(solution)/shard_map/ppermute | solution.py:349
  150.5 22.9 %attention_forward.1 = (f32[1024,1280]{1,0:T(8,128)}, bf16[4,10,768,256]{3,2,1,0:T(8,128)(2,1)}, f32[8,1024]{1,0:T(8,128)}) custom-call(s32[1744]{0:T(1024)S(1)} %get-tuple-element.327, bf16[1024,1280]{1,0:T(8,128)(2,1)} %q_ref.1, ...), custom_call_target="tpu_custom_call" | custom-call | flops 4026531840 | bytes 50000000 | tf_op jit(solution)/shard_map/attention_forward/pallas_call | solution.py:849
  179.2 30.4 %attention_backward.1 = (bf16[1024,1280]{1,0:T(8,128)(2,1)}, bf16[1024,1280]{1,0:T(8,128)(2,1)}, bf16[46,256,1280]{2,1,0:T(8,128)(2,1)}) custom-call(s32[1744]{0:T(1024)S(1)} %get-tuple-element.327, bf16[1024,1280]{1,0:T(8,128)(2,1)} %q_ref.1, ...), custom_call_target="tpu_custom_call", output_to_operand_aliasing={{2}: (2, {})} | custom-call | flops 8053063680 | bytes 70000000 | tf_op jit(solution)/shard_map/attention_backward/pallas_call | solution.py:880
  211.7 4.6 %collective-permute-start.37 = (bf16[256,1280]{1,0:T(8,128)(2,1)}, bf16[256,1280]{1,0:T(8,128)(2,1)S(1)}, u32[]{:S(2)}, u32[]{:S(2)}) collective-permute-start(bf16[256,1280]{1,0:T(8,128)(2,1)} %get-tuple-element.194), channel_id=1, source_target_pairs={{0,8},{4,12},{8,16},{12,20},{16,24},{20,28},{1,9},{5,13},{9,17},{1... | collective-permute-start | bytes 1966088 | tf_op jit(solution)/shard_map/ppermute | solution.py:349
  221.1 4.6 %collective-permute-start.40 = (bf16[256,1280]{1,0:T(8,128)(2,1)}, bf16[256,1280]{1,0:T(8,128)(2,1)S(1)}, u32[]{:S(2)}, u32[]{:S(2)}) collective-permute-start(bf16[256,1280]{1,0:T(8,128)(2,1)} %get-tuple-element.198), channel_id=1, source_target_pairs={{0,8},{4,12},{8,16},{12,20},{16,24},{20,28},{1,9},{5,13},{9,17},{1... | collective-permute-start | bytes 1966088 | tf_op jit(solution)/shard_map/ppermute | solution.py:349
  240.2 4.6 %collective-permute-start.43 = (bf16[256,1280]{1,0:T(8,128)(2,1)}, bf16[256,1280]{1,0:T(8,128)(2,1)S(1)}, u32[]{:S(2)}, u32[]{:S(2)}) collective-permute-start(bf16[256,1280]{1,0:T(8,128)(2,1)} %get-tuple-element.202), channel_id=1, source_target_pairs={{0,8},{4,12},{8,16},{12,20},{16,24},{20,28},{1,9},{5,13},{9,17},{1... | collective-permute-start | bytes 1966088 | tf_op jit(solution)/shard_map/ppermute | solution.py:349
  252.0 6.8 %collective-permute-start.46 = (bf16[256,1280]{1,0:T(8,128)(2,1)}, bf16[256,1280]{1,0:T(8,128)(2,1)S(1)}, u32[]{:S(2)}, u32[]{:S(2)}) collective-permute-start(bf16[256,1280]{1,0:T(8,128)(2,1)} %get-tuple-element.206), channel_id=1, source_target_pairs={{0,8},{4,12},{8,16},{12,20},{16,24},{20,28},{1,9},{5,13},{9,17},{1... | collective-permute-start | bytes 1966088 | tf_op jit(solution)/shard_map/ppermute | solution.py:349
  268.3 5.5 %collective-permute-start.49 = (bf16[256,1280]{1,0:T(8,128)(2,1)}, bf16[256,1280]{1,0:T(8,128)(2,1)S(1)}, u32[]{:S(2)}, u32[]{:S(2)}) collective-permute-start(bf16[256,1280]{1,0:T(8,128)(2,1)} %get-tuple-element.210), channel_id=1, source_target_pairs={{0,8},{4,12},{8,16},{12,20},{16,24},{20,28},{1,9},{5,13},{9,17},{1... | collective-permute-start | bytes 1966088 | tf_op jit(solution)/shard_map/ppermute | solution.py:349
  280.1 6.8 %collective-permute-start.52 = (bf16[256,1280]{1,0:T(8,128)(2,1)}, bf16[256,1280]{1,0:T(8,128)(2,1)S(1)}, u32[]{:S(2)}, u32[]{:S(2)}) collective-permute-start(bf16[256,1280]{1,0:T(8,128)(2,1)} %get-tuple-element.214), channel_id=1, source_target_pairs={{0,8},{4,12},{8,16},{12,20},{16,24},{20,28},{1,9},{5,13},{9,17},{1... | collective-permute-start | bytes 1966088 | tf_op jit(solution)/shard_map/ppermute | solution.py:349
  296.4 6.5 %collective-permute-start.55 = (bf16[256,1280]{1,0:T(8,128)(2,1)}, bf16[256,1280]{1,0:T(8,128)(2,1)S(1)}, u32[]{:S(2)}, u32[]{:S(2)}) collective-permute-start(bf16[256,1280]{1,0:T(8,128)(2,1)} %get-tuple-element.218), channel_id=1, source_target_pairs={{0,8},{4,12},{8,16},{12,20},{16,24},{20,28},{1,9},{5,13},{9,17},{1... | collective-permute-start | bytes 1966088 | tf_op jit(solution)/shard_map/ppermute | solution.py:349
  311.5 4.6 %collective-permute-start.58 = (bf16[256,1280]{1,0:T(8,128)(2,1)}, bf16[256,1280]{1,0:T(8,128)(2,1)S(1)}, u32[]{:S(2)}, u32[]{:S(2)}) collective-permute-start(bf16[256,1280]{1,0:T(8,128)(2,1)} %get-tuple-element.222), channel_id=1, source_target_pairs={{0,8},{4,12},{8,16},{12,20},{16,24},{20,28},{1,9},{5,13},{9,17},{1... | collective-permute-start | bytes 1966088 | tf_op jit(solution)/shard_map/ppermute | solution.py:349
  326.3 4.8 %collective-permute-start.61 = (bf16[256,1280]{1,0:T(8,128)(2,1)}, bf16[256,1280]{1,0:T(8,128)(2,1)S(1)}, u32[]{:S(2)}, u32[]{:S(2)}) collective-permute-start(bf16[256,1280]{1,0:T(8,128)(2,1)} %get-tuple-element.225), channel_id=1, source_target_pairs={{0,8},{4,12},{8,16},{12,20},{16,24},{20,28},{1,9},{5,13},{9,17},{1... | collective-permute-start | bytes 1966088 | tf_op jit(solution)/shard_map/ppermute | solution.py:349
  334.6 5.8 %collective-permute-done.60.refs_3_ = bf16[256,1280]{1,0:T(8,128)(2,1)S(1)} collective-permute-done((bf16[256,1280]{1,0:T(8,128)(2,1)}, bf16[256,1280]{1,0:T(8,128)(2,1)S(1)}, u32[]{:S(2)}, u32[]{:S(2)}) %collective-permute-start.60) | collective-permute-done | bytes 655392 | tf_op jit(solution)/shard_map/ppermute | solution.py:349
  346.1 6.6 %return_home.1 = (bf16[4,256,1280]{2,1,0:T(8,128)(2,1)}, bf16[4,256,1280]{2,1,0:T(8,128)(2,1)}) custom-call(s32[1744]{0:T(1024)S(1)} %get-tuple-element.328, bf16[46,256,1280]{2,1,0:T(8,128)(2,1)} %get-tuple-element.220.pool_ref, bf16[256,1280]{1,0:T(8,128)(2,1)} %copy-done.11, bf16[256,1280]{1,0:T(8,128)(2,1)} %copy-done.12, bf16[256,1280]{1,0:T(8,128)(2,1)} %copy-done.14, ...), custom_call_target="tpu_custom_call" | custom-call | bytes 19660800 | tf_op jit(solution)/shard_map/return_home/pallas_call | solution.py:589
  (235 shorter events, 179.5 us)
Async XLA Ops:
  10.9 20.4 %collective-permute-start.6 = (bf16[256,1280]{1,0:T(8,128)(2,1)}, bf16[256,1280]{1,0:T(8,128)(2,1)S(1)}, u32[]{:S(2)}, u32[]{:S(2)}) collective-permute-start(bf16[256,1280]{1,0:T(8,128)(2,1)} %get-tuple-element.150), channel_id=1, source_target_pairs={{0,8},{4,12},{8,16},{12,20},{16,24},{20,28},{1,9},{5,13},{9,17},{1... | collective-permute-start | bytes 1966088 | tf_op jit(solution)/shard_map/ppermute | solution.py:349
  15.9 21.7 %collective-permute-start.7 = (bf16[256,1280]{1,0:T(8,128)(2,1)}, bf16[256,1280]{1,0:T(8,128)(2,1)S(1)}, u32[]{:S(2)}, u32[]{:S(2)}) collective-permute-start(bf16[256,1280]{1,0:T(8,128)(2,1)} %get-tuple-element.151), channel_id=1, source_target_pairs={{8,0},{12,4},{16,8},{20,12},{24,16},{28,20},{9,1},{13,5},{17,9},{2... | collective-permute-start | bytes 1966088 | tf_op jit(solution)/shard_map/ppermute | solution.py:349
  17.2 20.4 %collective-permute-start.8 = (bf16[256,1280]{1,0:T(8,128)(2,1)}, bf16[256,1280]{1,0:T(8,128)(2,1)S(1)}, u32[]{:S(2)}, u32[]{:S(2)}) collective-permute-start(bf16[256,1280]{1,0:T(8,128)(2,1)} %get-tuple-element.152), channel_id=1, source_target_pairs={{0,4},{4,0},{8,12},{12,8},{16,20},{20,16},{24,28},{28,24},{1,5},{5... | collective-permute-start | bytes 1966088 | tf_op jit(solution)/shard_map/ppermute | solution.py:349
  21.4 27.0 %collective-permute-start.9 = (bf16[256,1280]{1,0:T(8,128)(2,1)}, bf16[256,1280]{1,0:T(8,128)(2,1)S(1)}, u32[]{:S(2)}, u32[]{:S(2)}) collective-permute-start(bf16[256,1280]{1,0:T(8,128)(2,1)} %get-tuple-element.154), channel_id=1, source_target_pairs={{0,8},{4,12},{8,16},{12,20},{16,24},{20,28},{1,9},{5,13},{9,17},{1... | collective-permute-start | bytes 1966088 | tf_op jit(solution)/shard_map/ppermute | solution.py:349
  26.4 23.3 %collective-permute-start.10 = (bf16[256,1280]{1,0:T(8,128)(2,1)}, bf16[256,1280]{1,0:T(8,128)(2,1)S(1)}, u32[]{:S(2)}, u32[]{:S(2)}) collective-permute-start(bf16[256,1280]{1,0:T(8,128)(2,1)} %get-tuple-element.155), channel_id=1, source_target_pairs={{8,0},{12,4},{16,8},{20,12},{24,16},{28,20},{9,1},{13,5},{17,9},{2... | collective-permute-start | bytes 1966088 | tf_op jit(solution)/shard_map/ppermute | solution.py:349
  54.1 24.1 %collective-permute-start.15 = (bf16[256,1280]{1,0:T(8,128)(2,1)}, bf16[256,1280]{1,0:T(8,128)(2,1)S(1)}, u32[]{:S(2)}, u32[]{:S(2)}) collective-permute-start(bf16[256,1280]{1,0:T(8,128)(2,1)} %get-tuple-element.162), channel_id=1, source_target_pairs={{0,8},{4,12},{8,16},{12,20},{16,24},{20,28},{1,9},{5,13},{9,17},{1... | collective-permute-start | bytes 1966088 | tf_op jit(solution)/shard_map/ppermute | solution.py:349
  58.4 23.1 %collective-permute-start.16 = (bf16[256,1280]{1,0:T(8,128)(2,1)}, bf16[256,1280]{1,0:T(8,128)(2,1)S(1)}, u32[]{:S(2)}, u32[]{:S(2)}) collective-permute-start(bf16[256,1280]{1,0:T(8,128)(2,1)} %get-tuple-element.163), channel_id=1, source_target_pairs={{8,0},{12,4},{16,8},{20,12},{24,16},{28,20},{9,1},{13,5},{17,9},{2... | collective-permute-start | bytes 1966088 | tf_op jit(solution)/shard_map/ppermute | solution.py:349
  83.4 23.2 %collective-permute-start.21 = (bf16[256,1280]{1,0:T(8,128)(2,1)}, bf16[256,1280]{1,0:T(8,128)(2,1)S(1)}, u32[]{:S(2)}, u32[]{:S(2)}) collective-permute-start(bf16[256,1280]{1,0:T(8,128)(2,1)} %get-tuple-element.170), channel_id=1, source_target_pairs={{0,8},{4,12},{8,16},{12,20},{16,24},{20,28},{1,9},{5,13},{9,17},{1... | collective-permute-start | bytes 1966088 | tf_op jit(solution)/shard_map/ppermute | solution.py:349
  89.8 20.8 %collective-permute-start.22 = (bf16[256,1280]{1,0:T(8,128)(2,1)}, bf16[256,1280]{1,0:T(8,128)(2,1)S(1)}, u32[]{:S(2)}, u32[]{:S(2)}) collective-permute-start(bf16[256,1280]{1,0:T(8,128)(2,1)} %get-tuple-element.171), channel_id=1, source_target_pairs={{8,0},{12,4},{16,8},{20,12},{24,16},{28,20},{9,1},{13,5},{17,9},{2... | collective-permute-start | bytes 1966088 | tf_op jit(solution)/shard_map/ppermute | solution.py:349
  112.5 21.8 %collective-permute-start.27 = (bf16[256,1280]{1,0:T(8,128)(2,1)}, bf16[256,1280]{1,0:T(8,128)(2,1)S(1)}, u32[]{:S(2)}, u32[]{:S(2)}) collective-permute-start(bf16[256,1280]{1,0:T(8,128)(2,1)} %get-tuple-element.178), channel_id=1, source_target_pairs={{0,8},{4,12},{8,16},{12,20},{16,24},{20,28},{1,9},{5,13},{9,17},{1... | collective-permute-start | bytes 1966088 | tf_op jit(solution)/shard_map/ppermute | solution.py:349
  118.5 20.6 %collective-permute-start.28 = (bf16[256,1280]{1,0:T(8,128)(2,1)}, bf16[256,1280]{1,0:T(8,128)(2,1)S(1)}, u32[]{:S(2)}, u32[]{:S(2)}) collective-permute-start(bf16[256,1280]{1,0:T(8,128)(2,1)} %get-tuple-element.179), channel_id=1, source_target_pairs={{8,0},{12,4},{16,8},{20,12},{24,16},{28,20},{9,1},{13,5},{17,9},{2... | collective-permute-start | bytes 1966088 | tf_op jit(solution)/shard_map/ppermute | solution.py:349
  211.7 21.2 %collective-permute-start.37 = (bf16[256,1280]{1,0:T(8,128)(2,1)}, bf16[256,1280]{1,0:T(8,128)(2,1)S(1)}, u32[]{:S(2)}, u32[]{:S(2)}) collective-permute-start(bf16[256,1280]{1,0:T(8,128)(2,1)} %get-tuple-element.194), channel_id=1, source_target_pairs={{0,8},{4,12},{8,16},{12,20},{16,24},{20,28},{1,9},{5,13},{9,17},{1... | collective-permute-start | bytes 1966088 | tf_op jit(solution)/shard_map/ppermute | solution.py:349
  219.8 25.0 %collective-permute-start.39 = (bf16[256,1280]{1,0:T(8,128)(2,1)}, bf16[256,1280]{1,0:T(8,128)(2,1)S(1)}, u32[]{:S(2)}, u32[]{:S(2)}) collective-permute-start(bf16[256,1280]{1,0:T(8,128)(2,1)} %get-tuple-element.197), channel_id=1, source_target_pairs={{8,0},{12,4},{16,8},{20,12},{24,16},{28,20},{9,1},{13,5},{17,9},{2... | collective-permute-start | bytes 1966088 | tf_op jit(solution)/shard_map/ppermute | solution.py:349
  221.1 25.9 %collective-permute-start.40 = (bf16[256,1280]{1,0:T(8,128)(2,1)}, bf16[256,1280]{1,0:T(8,128)(2,1)S(1)}, u32[]{:S(2)}, u32[]{:S(2)}) collective-permute-start(bf16[256,1280]{1,0:T(8,128)(2,1)} %get-tuple-element.198), channel_id=1, source_target_pairs={{0,8},{4,12},{8,16},{12,20},{16,24},{20,28},{1,9},{5,13},{9,17},{1... | collective-permute-start | bytes 1966088 | tf_op jit(solution)/shard_map/ppermute | solution.py:349
  240.2 20.8 %collective-permute-start.43 = (bf16[256,1280]{1,0:T(8,128)(2,1)}, bf16[256,1280]{1,0:T(8,128)(2,1)S(1)}, u32[]{:S(2)}, u32[]{:S(2)}) collective-permute-start(bf16[256,1280]{1,0:T(8,128)(2,1)} %get-tuple-element.202), channel_id=1, source_target_pairs={{0,8},{4,12},{8,16},{12,20},{16,24},{20,28},{1,9},{5,13},{9,17},{1... | collective-permute-start | bytes 1966088 | tf_op jit(solution)/shard_map/ppermute | solution.py:349
  250.7 23.2 %collective-permute-start.45 = (bf16[256,1280]{1,0:T(8,128)(2,1)}, bf16[256,1280]{1,0:T(8,128)(2,1)S(1)}, u32[]{:S(2)}, u32[]{:S(2)}) collective-permute-start(bf16[256,1280]{1,0:T(8,128)(2,1)} %get-tuple-element.205), channel_id=1, source_target_pairs={{8,0},{12,4},{16,8},{20,12},{24,16},{28,20},{9,1},{13,5},{17,9},{2... | collective-permute-start | bytes 1966088 | tf_op jit(solution)/shard_map/ppermute | solution.py:349
  252.0 23.0 %collective-permute-start.46 = (bf16[256,1280]{1,0:T(8,128)(2,1)}, bf16[256,1280]{1,0:T(8,128)(2,1)S(1)}, u32[]{:S(2)}, u32[]{:S(2)}) collective-permute-start(bf16[256,1280]{1,0:T(8,128)(2,1)} %get-tuple-element.206), channel_id=1, source_target_pairs={{0,8},{4,12},{8,16},{12,20},{16,24},{20,28},{1,9},{5,13},{9,17},{1... | collective-permute-start | bytes 1966088 | tf_op jit(solution)/shard_map/ppermute | solution.py:349
  268.3 21.6 %collective-permute-start.49 = (bf16[256,1280]{1,0:T(8,128)(2,1)}, bf16[256,1280]{1,0:T(8,128)(2,1)S(1)}, u32[]{:S(2)}, u32[]{:S(2)}) collective-permute-start(bf16[256,1280]{1,0:T(8,128)(2,1)} %get-tuple-element.210), channel_id=1, source_target_pairs={{0,8},{4,12},{8,16},{12,20},{16,24},{20,28},{1,9},{5,13},{9,17},{1... | collective-permute-start | bytes 1966088 | tf_op jit(solution)/shard_map/ppermute | solution.py:349
  278.8 24.1 %collective-permute-start.51 = (bf16[256,1280]{1,0:T(8,128)(2,1)}, bf16[256,1280]{1,0:T(8,128)(2,1)S(1)}, u32[]{:S(2)}, u32[]{:S(2)}) collective-permute-start(bf16[256,1280]{1,0:T(8,128)(2,1)} %get-tuple-element.213), channel_id=1, source_target_pairs={{8,0},{12,4},{16,8},{20,12},{24,16},{28,20},{9,1},{13,5},{17,9},{2... | collective-permute-start | bytes 1966088 | tf_op jit(solution)/shard_map/ppermute | solution.py:349
  280.1 24.4 %collective-permute-start.52 = (bf16[256,1280]{1,0:T(8,128)(2,1)}, bf16[256,1280]{1,0:T(8,128)(2,1)S(1)}, u32[]{:S(2)}, u32[]{:S(2)}) collective-permute-start(bf16[256,1280]{1,0:T(8,128)(2,1)} %get-tuple-element.214), channel_id=1, source_target_pairs={{0,8},{4,12},{8,16},{12,20},{16,24},{20,28},{1,9},{5,13},{9,17},{1... | collective-permute-start | bytes 1966088 | tf_op jit(solution)/shard_map/ppermute | solution.py:349
  295.1 21.1 %collective-permute-start.54 = (bf16[256,1280]{1,0:T(8,128)(2,1)}, bf16[256,1280]{1,0:T(8,128)(2,1)S(1)}, u32[]{:S(2)}, u32[]{:S(2)}) collective-permute-start(bf16[256,1280]{1,0:T(8,128)(2,1)} %get-tuple-element.217), channel_id=1, source_target_pairs={{8,0},{12,4},{16,8},{20,12},{24,16},{28,20},{9,1},{13,5},{17,9},{2... | collective-permute-start | bytes 1966088 | tf_op jit(solution)/shard_map/ppermute | solution.py:349
  296.4 22.0 %collective-permute-start.55 = (bf16[256,1280]{1,0:T(8,128)(2,1)}, bf16[256,1280]{1,0:T(8,128)(2,1)S(1)}, u32[]{:S(2)}, u32[]{:S(2)}) collective-permute-start(bf16[256,1280]{1,0:T(8,128)(2,1)} %get-tuple-element.218), channel_id=1, source_target_pairs={{0,8},{4,12},{8,16},{12,20},{16,24},{20,28},{1,9},{5,13},{9,17},{1... | collective-permute-start | bytes 1966088 | tf_op jit(solution)/shard_map/ppermute | solution.py:349
  310.2 20.9 %collective-permute-start.57 = (bf16[256,1280]{1,0:T(8,128)(2,1)}, bf16[256,1280]{1,0:T(8,128)(2,1)S(1)}, u32[]{:S(2)}, u32[]{:S(2)}) collective-permute-start(bf16[256,1280]{1,0:T(8,128)(2,1)} %get-tuple-element.221), channel_id=1, source_target_pairs={{8,0},{12,4},{16,8},{20,12},{24,16},{28,20},{9,1},{13,5},{17,9},{2... | collective-permute-start | bytes 1966088 | tf_op jit(solution)/shard_map/ppermute | solution.py:349
  311.5 21.5 %collective-permute-start.58 = (bf16[256,1280]{1,0:T(8,128)(2,1)}, bf16[256,1280]{1,0:T(8,128)(2,1)S(1)}, u32[]{:S(2)}, u32[]{:S(2)}) collective-permute-start(bf16[256,1280]{1,0:T(8,128)(2,1)} %get-tuple-element.222), channel_id=1, source_target_pairs={{0,8},{4,12},{8,16},{12,20},{16,24},{20,28},{1,9},{5,13},{9,17},{1... | collective-permute-start | bytes 1966088 | tf_op jit(solution)/shard_map/ppermute | solution.py:349
  (89 other events, 708.8 us)
